TPU v7x, 128 devices: a whole 4x4x4 slice. The times are simulated.
128 devices in a mesh: ep: 32 (over x, y, core), th: 4 (over z).
Axes of the slice: x: 4, y: 4, z: 4, core: 2. Of those that a mesh axis runs over, the one named last changes fastest.
Arguments:
- tokens: bfloat16 [4096, 4096], P('ep', 'th'), may hold values from -6 to 6
- cotangent: bfloat16 [4096, 4096], P('ep', 'th'), may hold values from -6 to 6
- gates: bfloat16 [4096, 8], P('ep'), may hold values from 0.049804688 to 0.5
- routing: int32 [4096, 8], P('ep'), may hold values from 0 to 31, all different within a row; in each aligned block of 128 rows (0 to 127, 128 to 255, ...) at most 36 rows name the same one
- new_slot: int32 [32], replicated, may hold values from 0 to 31, each once
- gate_old: bfloat16 [32, 4096, 1536], P(None, 'ep', 'th'), may hold values from -0.09375 to 0.09375
- up_old: bfloat16 [32, 4096, 1536], P(None, 'ep', 'th'), may hold values from -0.09375 to 0.09375
- down_old: bfloat16 [32, 4096, 1536], P(None, 'ep', 'th'), may hold values from -0.15625 to 0.15625
Outputs:
- grad_tokens: bfloat16 [4096, 4096], P('ep', 'th')
- grad_gates: bfloat16 [4096, 8], P('ep')
- grad_gate_w: bfloat16 [32, 4096, 1536], P('ep', None, 'th')
- grad_up_w: bfloat16 [32, 4096, 1536], P('ep', None, 'th')
- grad_down_w: bfloat16 [32, 4096, 1536], P('ep', None, 'th')
Inputs may be any that keep to these rules, and one draw needn't show every extreme that they name: `routing`: each row names 8 different experts; among the rows of one device (128 aligned rows) no expert is named by more than 36 rows, and one expert is named by exactly 36 in some blocks. `new_slot`: each compacted id stands once.
All inputs are finite; a program needn't handle non-finite values.
Results may differ from a plain program's by a relative error of at most 0.015.
Values may be sent and summed in bfloat16 or wider, within the bound.
A program may use at most 192 MiB of HBM per device.

v0:
```python
import jax
import jax.numpy as jnp
from jax import lax
from jax.sharding import PartitionSpec as P

CAP = 36


def local(tokens, cotangent, gates, routing, new_slot, gate_old, up_old, down_old):
    ep_count = lax.axis_size("ep")
    expert_total = new_slot.shape[0]
    per_device = expert_total // ep_count
    tok_count, top_count = routing.shape
    capacity = CAP
    slot_count = expert_total * capacity
    expert_ids = jnp.arange(expert_total, dtype=jnp.int32)
    hit_map = (new_slot[None, :] == expert_ids[:, None]).astype(jnp.int32)
    inverse = jnp.sum(hit_map * expert_ids[None, :], axis=1)
    w_gate, w_up, w_down = (
        lax.all_to_all(
            jnp.take(gate_old, inverse, axis=0), "ep", split_axis=0, concat_axis=1, tiled=True
        ),
        lax.all_to_all(
            jnp.take(up_old, inverse, axis=0), "ep", split_axis=0, concat_axis=1, tiled=True
        ),
        lax.all_to_all(
            jnp.take(down_old, inverse, axis=0), "ep", split_axis=0, concat_axis=1, tiled=True
        ),
    )
    flat_route = routing.reshape(-1)
    hit_table = (flat_route[:, None] == expert_ids[None, :]).astype(jnp.int32)
    earlier = jnp.cumsum(hit_table, axis=0) - hit_table
    slot_rank = jnp.sum(earlier * hit_table, axis=1)
    slot_index = flat_route * capacity + slot_rank
    entry_count = slot_index.shape[0]
    matches = slot_index[:, None] == jnp.arange(slot_count, dtype=jnp.int32)[None, :]
    filled = jnp.any(matches, axis=0)
    entry_index = jnp.sum(
        jnp.where(matches, jnp.arange(entry_count, dtype=jnp.int32)[:, None], 0), axis=0
    )
    token_index = entry_index // top_count
    live = filled[:, None].astype(jnp.bfloat16)
    gate_send = gates.reshape(-1)[entry_index] * filled.astype(jnp.bfloat16)
    full_tokens, full_cot = (
        lax.all_gather(tokens, "th", axis=1, tiled=True),
        lax.all_gather(cotangent, "th", axis=1, tiled=True),
    )
    rows_in, rows_grad, gate_recv = (
        lax.all_to_all(
            full_tokens[token_index] * live, "ep", split_axis=0, concat_axis=0, tiled=True
        ),
        lax.all_to_all(full_cot[token_index] * live, "ep", split_axis=0, concat_axis=0, tiled=True),
        lax.all_to_all(gate_send, "ep", split_axis=0, concat_axis=0, tiled=True),
    )
    width = rows_in.shape[1]
    shaped_in = rows_in.reshape(ep_count, per_device, capacity, width)
    shaped_grad = rows_grad.reshape(ep_count, per_device, capacity, width)
    weight_g = gate_recv.astype(jnp.float32).reshape(ep_count, per_device, capacity, 1)
    gate_pre = jnp.einsum("secd,edf->secf", shaped_in, w_gate, preferred_element_type=jnp.float32)
    up_pre = jnp.einsum("secd,edf->secf", shaped_in, w_up, preferred_element_type=jnp.float32)
    back_hid = jnp.einsum("secd,edf->secf", shaped_grad, w_down, preferred_element_type=jnp.float32)
    sigmoid_gate = jax.nn.sigmoid(gate_pre)
    silu_gate = gate_pre * sigmoid_gate
    hidden = silu_gate * up_pre
    grad_hid = weight_g * back_hid
    grad_gate_pre = (
        grad_hid * up_pre * sigmoid_gate * (1.0 + gate_pre * (1.0 - sigmoid_gate))
    ).astype(jnp.bfloat16)
    grad_up_pre = (grad_hid * silu_gate).astype(jnp.bfloat16)
    scaled_hidden = (weight_g * hidden).astype(jnp.bfloat16)
    router_part = jnp.sum(back_hid * hidden, axis=3)
    grad_wg = jnp.einsum(
        "secd,secf->edf", shaped_in, grad_gate_pre, preferred_element_type=jnp.float32
    ).astype(jnp.bfloat16)
    grad_wu = jnp.einsum(
        "secd,secf->edf", shaped_in, grad_up_pre, preferred_element_type=jnp.float32
    ).astype(jnp.bfloat16)
    grad_wd = jnp.einsum(
        "secd,secf->edf", shaped_grad, scaled_hidden, preferred_element_type=jnp.float32
    ).astype(jnp.bfloat16)
    router_term = lax.psum(router_part, "th").reshape(-1).astype(jnp.bfloat16)
    partial_value = jnp.einsum(
        "secf,edf->secd", grad_gate_pre, w_gate, preferred_element_type=jnp.float32
    )
    partial_value = partial_value + jnp.einsum(
        "secf,edf->secd", grad_up_pre, w_up, preferred_element_type=jnp.float32
    )
    partial_bf = partial_value.reshape(-1, width).astype(jnp.bfloat16)
    rounded = lax.optimization_barrier(partial_bf).astype(jnp.float32)
    slot_grad = lax.psum_scatter(
        rounded.astype(jnp.bfloat16), "th", scatter_dimension=1, tiled=True
    )
    back_rows, back_router = (
        lax.all_to_all(slot_grad, "ep", split_axis=0, concat_axis=0, tiled=True),
        lax.all_to_all(router_term, "ep", split_axis=0, concat_axis=0, tiled=True),
    )
    entry_grad = back_rows[slot_index]
    slice_width = entry_grad.shape[1]
    grad_tokens = jnp.sum(
        entry_grad.astype(jnp.float32).reshape(tok_count, top_count, slice_width), axis=1
    ).astype(jnp.bfloat16)
    grad_gates = back_router[slot_index].reshape(tok_count, top_count)
    return (grad_tokens, grad_gates, grad_wg, grad_wu, grad_wd)


def solution(mesh):
    placed = (
        P("ep", "th"),
        P("ep", "th"),
        P("ep", None),
        P("ep", None),
        P(),
        P(None, "ep", "th"),
        P(None, "ep", "th"),
        P(None, "ep", "th"),
    )
    return jax.shard_map(
        local,
        mesh=mesh,
        in_specs=placed,
        out_specs=(
            P("ep", "th"),
            P("ep", None),
            P("ep", None, "th"),
            P("ep", None, "th"),
            P("ep", None, "th"),
        ),
        check_vma=False,
    )
```

profile of v0, /device:TPU:1, one launch (start us, length us, event | category | flops | bytes accessed | tf_op | source)
XLA Modules:
  0.0 732.7 jit_solution(6436824649356158833)
XLA Ops:
  7.2 0.9 copy.36
  8.3 9.0 %reduce-window.6 = s32[32,8,128]{2,1,0:T(8,128)S(1)} reduce-window(s32[32,8,128]{2,1,0:T(8,128)S(1)} %fusion.23, s32[]{:T(128)} %constant.25.clone.1), window={size=1x1x128 pad=0_0x0_0x127_0}, to_apply=%region_1.0 | reduce-window | flops 4161536 | bytes 262148 | tf_op jit(solution)/shard_map/reduce-window
  17.9 0.6 copy-done.8
  18.5 0.7 fusion.4
  19.7 0.8 copy.40
  20.7 7.3 gather_fusion
  28.0 0.7 mul.117
  28.7 8.6 %all-to-all-start.1 = ((bf16[32,36,1]{1,2,0:T(2,128)(2,1)}), bf16[32,36,1]{1,2,0:T(2,128)(2,1)S(1)}, u32[]{:S(2)}, u32[]{:S(2)}) async-start(bf16[32,36,1]{1,2,0:T(2,128)(2,1)} %mul.117), calls=%async_computation.1 | async-start | bytes 32768 | tf_op jit(solution)/shard_map/all_to_all | solution.py:53
  37.5 2.6 gather_fusion.7
  40.1 4.7 gather_fusion.6
  44.8 2.6 gather_fusion.5
  47.4 6.0 broadcast_select_fusion.1
  53.5 46.7 %all_to_all.66 = bf16[32,128,384]{2,1,0:T(8,128)(2,1)} all-to-all(bf16[32,128,384]{2,1,0:T(8,128)(2,1)S(1)} %get-tuple-element.33), channel_id=1, replica_groups=mesh['ep'=32,'th'=4] {'ep'}, dimensions={0} | all-to-all | bytes 6291456 | tf_op jit(solution)/shard_map/all_to_all | solution.py:26
  100.1 4.0 all-to-all-start.4
  104.1 0.7 all-gather.5.cloned.1.call-update
  104.9 0.7 all-gather.3.cloned.1.call-update
  105.6 38.3 %all-to-all-done.4 = bf16[32,128,384]{2,1,0:T(8,128)(2,1)S(1)} async-done(((bf16[32,128,384]{2,1,0:T(8,128)(2,1)}), bf16[32,128,384]{2,1,0:T(8,128)(2,1)S(1)}, u32[]{:S(2)}, u32[]{:S(2)}) %all-to-all-start.4) | async-done | bytes 3145760 | tf_op jit(solution)/shard_map/all_to_all | solution.py:23
  143.9 5.7 all-to-all-start
  149.8 19.7 %gather_fusion.2 = bf16[1152,4096]{1,0:T(8,128)(2,1)} fusion(bf16[128,4096]{1,0:T(8,128)(2,1)} %all-gather.5.cloned.1.call-done, s32[2048]{0:T(1024)S(1)} %pad_clamp_fusion), kind=kCustom, calls=%fused_computation.5 | custom fusion | bytes 18878976 | tf_op jit(solution)/shard_map/gather | solution.py:50
  169.5 13.2 %gather.28 = bf16[32,36,4096]{2,1,0:T(8,128)(2,1)} reshape(bf16[1152,4096]{1,0:T(8,128)(2,1)} %gather_fusion.2) | data formatting | bytes 18874368 | tf_op jit(solution)/shard_map/gather | solution.py:50
  182.6 19.8 %gather_fusion.1 = bf16[1152,4096]{1,0:T(8,128)(2,1)} fusion(bf16[128,4096]{1,0:T(8,128)(2,1)} %all-gather.3.cloned.1.call-done, s32[2048]{0:T(1024)S(1)} %pad_clamp_fusion), kind=kCustom, calls=%fused_computation.4 | custom fusion | bytes 18878976 | tf_op jit(solution)/shard_map/gather | solution.py:52
  202.4 13.1 %gather.26 = bf16[32,36,4096]{2,1,0:T(8,128)(2,1)} reshape(bf16[1152,4096]{1,0:T(8,128)(2,1)} %gather_fusion.1) | data formatting | bytes 18874368 | tf_op jit(solution)/shard_map/gather | solution.py:52
  215.6 15.9 %broadcast_multiply_fusion.1 = (bf16[32,36,4096]{2,1,0:T(8,128)(2,1)}, bf16[32,36,4096]{2,1,0:T(8,128)(2,1)}) fusion(bf16[32,36,4096]{2,1,0:T(8,128)(2,1)} %gather.26, bf16[32,36]{1,0:T(8,128)(2,1)S(1)} %reshape.294, bf16[32,36,4096]{2,1,0:T(8,128)(2,1)} %gather.28), kind=kLoop, calls=%fused_computation.14 | loop fusion | flops 9437184 | bytes 37751040 | tf_op jit(solution)/shard_map/mul | solution.py:52
  231.5 125.5 %all_to_all.67 = bf16[32,36,4096]{2,1,0:T(8,128)(2,1)} all-to-all(bf16[32,36,4096]{2,1,0:T(8,128)(2,1)} %get-tuple-element.32), channel_id=1, replica_groups=mesh['ep'=32,'th'=4] {'ep'}, dimensions={0} | all-to-all | bytes 18874368 | tf_op jit(solution)/shard_map/all_to_all | solution.py:49
  357.0 4.8 all-to-all-start.3
  362.1 10.4 %fusion.28 = f32[384,32,36]{0,2,1:T(8,128)} fusion(bf16[4096,384,1]{1,0,2:T(8,128)(2,1)} %bitcast.1, bf16[32,36,4096]{2,1,0:T(8,128)(2,1)} %all_to_all.67), kind=kOutput, calls=%fused_computation.79 | convolution fusion | flops 3623878656 | bytes 14352384 | tf_op jit(solution)/shard_map/secd,edf->secf/dot_general | solution.py:59
  372.5 7.0 fusion.27
  379.5 122.8 %all-to-all-done.3 = bf16[32,36,4096]{2,1,0:T(8,128)(2,1)} async-done(((bf16[32,36,4096]{2,1,0:T(8,128)(2,1)}), bf16[32,36,4096]{2,1,0:T(8,128)(2,1)}, u32[]{:S(2)}, u32[]{:S(2)}) %all-to-all-start.3) | async-done | bytes 9437216 | tf_op jit(solution)/shard_map/all_to_all | solution.py:52
  502.2 10.9 %fusion.8 = (f32[32,36]{1,0:T(8,128)S(1)}, bf16[32,1,36,384]{3,2,0,1:T(8,128)(2,1)S(1)}, bf16[32,36,384]{2,1,0:T(8,128)(2,1)S(1)}) fusion(f32[384,32,36]{0,2,1:T(8,128)} %fusion.27, f32[384,32,36]{0,2,1:T(8,128)} %fusion.28, f32[32,36]{1,0:T(8,128)S(1)} %bitcast.150, bf16[4096,384,1]{1,0,2:T(8,128)(2,1)} %bitcast.143, bf16[32,36,4096]{2,1,0:T(8,128)(2,1)} %all-to-all-done.3), kind=kOutput, calls=%fused_computation.32 | convolution fusion | flops 3631397888 | bytes 17900544 | tf_op jit(solution)/shard_map/secd,edf->secf/dot_general | solution.py:61
  513.2 12.5 %fusion.17 = f32[4096,32,36]{0,2,1:T(8,128)} fusion(bf16[4096,384,1]{1,0,2:T(8,128)(2,1)} %bitcast.1, bf16[32,1,36,384]{3,2,0,1:T(8,128)(2,1)S(1)} %get-tuple-element.29), kind=kOutput, calls=%fused_computation.45 | convolution fusion | flops 3623878656 | bytes 22904832 | tf_op jit(solution)/shard_map/secf,edf->secd/dot_general | solution.py:82
  525.7 12.4 %fusion = bf16[32,1,36,4096]{3,2,0,1:T(8,128)(2,1)} fusion(f32[4096,32,36]{0,2,1:T(8,128)} %fusion.17, bf16[4096,384,1]{1,0,2:T(8,128)(2,1)S(1)} %bitcast.142, bf16[32,36,384]{2,1,0:T(8,128)(2,1)S(1)} %get-tuple-element.30), kind=kOutput, calls=%fused_computation.9 | convolution fusion | flops 3633315840 | bytes 32342016 | tf_op jit(solution)/shard_map/secf,edf->secd/dot_general | solution.py:85
  538.1 13.3 %convert_element_type.98 = bf16[1152,4096]{1,0:T(8,128)(2,1)} reshape(bf16[32,1,36,4096]{3,2,0,1:T(8,128)(2,1)} %fusion) | data formatting | bytes 18874368 | tf_op jit(solution)/shard_map/convert_element_type | solution.py:88
  551.4 0.7 copy-done.10
  552.3 14.4 %psum.7 = bf16[32,1,36]{2,0,1:T(8,128)(2,1)S(1)} all-reduce(f32[32,1,36]{2,0,1:T(8,128)S(1)} %bitcast.149), channel_id=1, replica_groups=mesh['ep'=32,'th'=4] {'th'}, use_global_device_ids=true, to_apply=%region_9.11 | all-reduce | flops 1152 | bytes 6912 | tf_op jit(solution)/shard_map/psum | solution.py:81
  566.8 0.6 copy.43
  567.4 34.6 %all-to-all-start.7 = ((bf16[32,36,1]{1,2,0:T(2,128)(2,1)}), bf16[32,36,1]{1,2,0:T(2,128)(2,1)S(1)}, u32[]{:S(2)}, u32[]{:S(2)}) async-start(bf16[32,36,1]{1,2,0:T(2,128)(2,1)} %copy.43), calls=%async_computation.8 | async-start | bytes 32768 | tf_op jit(solution)/shard_map/all_to_all | solution.py:95
  602.0 11.0 %fusion.1 = bf16[1,4096,384]{2,1,0:T(8,128)(2,1)} fusion(bf16[32,36,4096]{2,1,0:T(8,128)(2,1)} %all_to_all.67, bf16[32,1,36,384]{3,2,0,1:T(8,128)(2,1)S(1)} %copy-done.7), kind=kOutput, calls=%fused_computation.15 | convolution fusion | flops 3625451520 | bytes 13467648 | tf_op jit(solution)/shard_map/secd,secf->edf/dot_general | solution.py:72
  613.1 10.8 %fusion.2 = bf16[1,4096,384]{2,1,0:T(8,128)(2,1)} fusion(bf16[32,36,4096]{2,1,0:T(8,128)(2,1)} %all_to_all.67, bf16[32,36,384]{2,1,0:T(8,128)(2,1)S(1)} %copy-done.5), kind=kOutput, calls=%fused_computation.16 | convolution fusion | flops 3625451520 | bytes 13467648 | tf_op jit(solution)/shard_map/secd,secf->edf/dot_general | solution.py:75
  623.9 42.3 %reduce-scatter.2.cloned.1.call-done = bf16[1152,1024]{1,0:T(8,128)(2,1)} async-done(((bf16[1152,4096]{1,0:T(8,128)(2,1)}), bf16[1152,1024]{1,0:T(8,128)(2,1)}) %reduce-scatter.2.cloned.1.call-update) | async-done | bytes 2359312 | tf_op jit(solution)/shard_map/reduce_scatter | solution.py:90
  666.2 4.1 all_to_all.53
  670.3 7.8 %all-to-all-start.6 = ((bf16[32,36,1024]{2,1,0:T(8,128)(2,1)}), bf16[32,36,1024]{2,1,0:T(8,128)(2,1)S(1)}, u32[]{:S(2)}, u32[]{:S(2)}) async-start(bf16[32,36,1024]{2,1,0:T(8,128)(2,1)} %all_to_all.53), calls=%async_computation.7 | async-start | bytes 5242880 | tf_op jit(solution)/shard_map/all_to_all | solution.py:94
  678.1 11.0 %fusion.3 = bf16[1,4096,384]{2,1,0:T(8,128)(2,1)} fusion(bf16[32,36,4096]{2,1,0:T(8,128)(2,1)} %all-to-all-done.3, f32[32,36]{1,0:T(8,128)S(1)} %bitcast.151, f32[384,32,36]{0,2,1:T(8,128)} %fusion.27, f32[384,32,36]{0,2,1:T(8,128)} %fusion.28), kind=kOutput, calls=%fused_computation.17 | convolution fusion | flops 3628548096 | bytes 16126464 | tf_op jit(solution)/shard_map/secd,secf->edf/dot_general | solution.py:78
  689.3 6.8 gather_fusion.4
  696.2 0.7 copy.44
  696.8 15.1 %all-to-all-done.6 = bf16[32,36,1024]{2,1,0:T(8,128)(2,1)S(1)} async-done(((bf16[32,36,1024]{2,1,0:T(8,128)(2,1)}), bf16[32,36,1024]{2,1,0:T(8,128)(2,1)S(1)}, u32[]{:S(2)}, u32[]{:S(2)}) %all-to-all-start.6) | async-done | bytes 2359328 | tf_op jit(solution)/shard_map/all_to_all | solution.py:94
  711.9 2.1 all_to_all.55
  714.0 8.1 %gather_fusion.3 = bf16[1024,1024]{1,0:T(8,128)(2,1)} fusion(bf16[1152,1024]{1,0:T(8,128)(2,1)} %all_to_all.55, s32[1024]{0:T(1024)S(1)} %broadcast_clamp_fusion), kind=kCustom, calls=%fused_computation.6 | custom fusion | bytes 4198400 | tf_op jit(solution)/shard_map/gather | solution.py:97
  722.1 3.7 bitcast_reduce_fusion
  (63 shorter events, 2.5 us)
Async XLA Ops:
  7.2 30.3 %copy-start = (bf16[32,128,384]{2,1,0:T(8,128)(2,1)S(1)}, bf16[32,128,384]{2,1,0:T(8,128)(2,1)}, u32[]{:S(2)}) copy-start(bf16[32,128,384]{2,1,0:T(8,128)(2,1)} %param.16) | copy-start | bytes 9437188
  7.2 30.1 %copy-start.11 = (s32[32]{0:T(128)S(1)}, s32[32]{0:T(128)}, u32[]{:S(2)}) copy-start(s32[32]{0:T(128)} %param.14) | copy-start | bytes 388
  17.9 0.6 copy-start.8
  28.7 24.8 %all-to-all-start.1 = ((bf16[32,36,1]{1,2,0:T(2,128)(2,1)}), bf16[32,36,1]{1,2,0:T(2,128)(2,1)S(1)}, u32[]{:S(2)}, u32[]{:S(2)}) async-start(bf16[32,36,1]{1,2,0:T(2,128)(2,1)} %mul.117), calls=%async_computation.1 | async-start | bytes 32768 | tf_op jit(solution)/shard_map/all_to_all | solution.py:53
  40.1 4.7 copy-start.3
  100.1 43.7 %all-to-all-start.4 = ((bf16[32,128,384]{2,1,0:T(8,128)(2,1)}), bf16[32,128,384]{2,1,0:T(8,128)(2,1)S(1)}, u32[]{:S(2)}, u32[]{:S(2)}) async-start(bf16[32,128,384]{2,1,0:T(8,128)(2,1)} %get-tuple-element.34), calls=%async_computation.4 | async-start | bytes 6291456 | tf_op jit(solution)/shard_map/all_to_all | solution.py:23
  104.1 45.7 %all-gather.5.cloned.1.call-start = ((), (), s32[]{:S(2)}) async-start(), calls=%async_computation.10 | async-start | bytes 1310720 | tf_op jit(solution)/shard_map/all_gather | solution.py:45
  104.8 77.8 %all-gather.3.cloned.1.call-start = ((), (), s32[]{:S(2)}) async-start(), calls=%async_computation.9 | async-start | bytes 1310720 | tf_op jit(solution)/shard_map/all_gather | solution.py:46
  143.9 87.6 %all-to-all-start = ((bf16[32,128,384]{2,1,0:T(8,128)(2,1)}), bf16[32,128,384]{2,1,0:T(8,128)(2,1)}, u32[]{:S(2)}, u32[]{:S(2)}) async-start(bf16[32,128,384]{2,1,0:T(8,128)(2,1)} %get-tuple-element.35), calls=%async_computation | async-start | bytes 6291456 | tf_op jit(solution)/shard_map/all_to_all | solution.py:20
  357.0 145.2 %all-to-all-start.3 = ((bf16[32,36,4096]{2,1,0:T(8,128)(2,1)}), bf16[32,36,4096]{2,1,0:T(8,128)(2,1)}, u32[]{:S(2)}, u32[]{:S(2)}) async-start(bf16[32,36,4096]{2,1,0:T(8,128)(2,1)} %get-tuple-element.31), calls=%async_computation.3 | async-start | bytes 20971520 | tf_op jit(solution)/shard_map/all_to_all | solution.py:52
  361.8 304.4 %reduce-scatter.2.cloned.1.call-start = ((), (), s32[]{:S(2)}) async-start(), calls=%async_computation.11 | async-start | bytes 11796480 | tf_op jit(solution)/shard_map/reduce_scatter | solution.py:90
  362.1 10.4 %copy-start.2 = (bf16[32,36,4096]{2,1,0:T(8,128)(2,1)S(1)}, bf16[32,36,4096]{2,1,0:T(8,128)(2,1)}, u32[]{:S(2)}) copy-start(bf16[32,36,4096]{2,1,0:T(8,128)(2,1)} %all_to_all.67) | copy-start | bytes 28311556
  513.1 12.5 %copy-start.6 = (bf16[32,1,36,384]{3,2,0,1:T(8,128)(2,1)}, bf16[32,1,36,384]{3,2,0,1:T(8,128)(2,1)S(1)}, u32[]{:S(2)}) copy-start(bf16[32,1,36,384]{3,2,0,1:T(8,128)(2,1)S(1)} %get-tuple-element.29) | copy-start | bytes 2654212
  513.1 12.5 %copy-start.4 = (bf16[32,36,384]{2,1,0:T(8,128)(2,1)}, bf16[32,36,384]{2,1,0:T(8,128)(2,1)S(1)}, u32[]{:S(2)}) copy-start(bf16[32,36,384]{2,1,0:T(8,128)(2,1)S(1)} %get-tuple-element.30) | copy-start | bytes 2654212
  551.4 0.7 copy-start.10
  551.4 0.9 copy-start.9
  551.4 50.6 %copy-start.7 = (bf16[32,1,36,384]{3,2,0,1:T(8,128)(2,1)S(1)}, bf16[32,1,36,384]{3,2,0,1:T(8,128)(2,1)}, u32[]{:S(2)}) copy-start(bf16[32,1,36,384]{3,2,0,1:T(8,128)(2,1)} %copy-done.6) | copy-start | bytes 2654212
  567.4 102.9 %all-to-all-start.7 = ((bf16[32,36,1]{1,2,0:T(2,128)(2,1)}), bf16[32,36,1]{1,2,0:T(2,128)(2,1)S(1)}, u32[]{:S(2)}, u32[]{:S(2)}) async-start(bf16[32,36,1]{1,2,0:T(2,128)(2,1)} %copy.43), calls=%async_computation.8 | async-start | bytes 32768 | tf_op jit(solution)/shard_map/all_to_all | solution.py:95
  602.0 11.1 %copy-start.5 = (bf16[32,36,384]{2,1,0:T(8,128)(2,1)S(1)}, bf16[32,36,384]{2,1,0:T(8,128)(2,1)}, u32[]{:S(2)}) copy-start(bf16[32,36,384]{2,1,0:T(8,128)(2,1)} %copy-done.4) | copy-start | bytes 2654212
  670.3 41.6 %all-to-all-start.6 = ((bf16[32,36,1024]{2,1,0:T(8,128)(2,1)}), bf16[32,36,1024]{2,1,0:T(8,128)(2,1)S(1)}, u32[]{:S(2)}, u32[]{:S(2)}) async-start(bf16[32,36,1024]{2,1,0:T(8,128)(2,1)} %all_to_all.53), calls=%async_computation.7 | async-start | bytes 5242880 | tf_op jit(solution)/shard_map/all_to_all | solution.py:94
  714.0 11.9 %copy-start.1 = (bf16[32,128,384]{2,1,0:T(8,128)(2,1)S(1)}, bf16[32,128,384]{2,1,0:T(8,128)(2,1)}, u32[]{:S(2)}) copy-start(bf16[32,128,384]{2,1,0:T(8,128)(2,1)} %param.16) | copy-start | bytes 9437188
Sparse Core Ops, SparseCore 0:
  106.6 25.2 all-gather.4
  133.6 24.5 all-gather.2
  551.5 114.6 reduce-scatter.1
where the time goes:
time: 740 us; the launch traced here: 733 us
  waiting for transfers between devices  220 us (30%)
  blocking collectives  187 us (25%)
  local copies, waits for them, and re-layouts  124 us (17%)
  matrix products  86.1 us (12%)
  starting transfers between devices  65.8 us (9%)
  other arithmetic  36.4 us (5%)
  between operations  14.3 us (2%)
    all_to_all x1, blocking collectives, local(): lax.all_to_all(full_tokens[token_index] * live, 'ep', split_axis=0, conca...  126 us
    all_to_all x1, waiting for transfers between devices, local(): lax.all_to_all(full_cot[token_index] * live, 'ep', split_axis=0, concat_a...  123 us
    all_to_all x1, blocking collectives, local(): lax.all_to_all(jnp.take(down_old, inverse, axis=0), 'ep', split_axis=0, c...  46.7 us
    reduce_scatter x1, waiting for transfers between devices, local(): lax.psum_scatter(rounded.astype(jnp.bfloat16), 'th', scatter_dimension=1,...  42.3 us
    all_to_all x1, waiting for transfers between devices, local(): lax.all_to_all(jnp.take(up_old, inverse, axis=0), 'ep', split_axis=0, con...  38.3 us
    all_to_all x1, starting transfers between devices, local(): lax.all_to_all(router_term, 'ep', split_axis=0, concat_axis=0, tiled=True)  34.6 us
    gather x2, local copies, waits for them, and re-layouts, local(): full_cot[token_index] * live  32.9 us
    gather x2, local copies, waits for them, and re-layouts, local(): full_tokens[token_index] * live  32.9 us
  transfers between devices with their start and end apart: 9, of which 4 were waited for; matrix products, arithmetic and copies ran while one was open for 21% of the time, Pallas kernels for 0%

commit v1 on v0

v1 whole, which is shorter than its diff:
```python
import jax
import jax.numpy as jnp
from jax import lax
from jax.experimental import pallas as pl
from jax.experimental.pallas import tpu as pltpu
from jax.sharding import PartitionSpec as P

CAP = 36


def reorder_body(inverse, gate_ref, up_ref, down_ref, gate_out, up_out, down_out):
    del inverse
    gate_out[...] = gate_ref[...]
    up_out[...] = up_ref[...]
    down_out[...] = down_ref[...]


def reorder(inverse, gate_old, up_old, down_old):
    count, rows, cols = gate_old.shape
    read = pl.BlockSpec((1, rows, cols), lambda j, inv: (inv[j], 0, 0))
    write = pl.BlockSpec((1, rows, cols), lambda j, inv: (j, 0, 0))
    return pl.pallas_call(
        reorder_body,
        out_shape=[jax.ShapeDtypeStruct(gate_old.shape, gate_old.dtype)] * 3,
        grid_spec=pltpu.PrefetchScalarGridSpec(
            num_scalar_prefetch=1, grid=(count,), in_specs=[read] * 3, out_specs=[write] * 3
        ),
    )(inverse, gate_old, up_old, down_old)


def local(tokens, cotangent, gates, routing, new_slot, gate_old, up_old, down_old):
    expert_total = new_slot.shape[0]
    tok_count, top_count = routing.shape
    expert_ids = jnp.arange(expert_total, dtype=jnp.int32)
    inverse = jnp.sum(
        (new_slot[None, :] == expert_ids[:, None]).astype(jnp.int32) * expert_ids[None, :], axis=1
    )
    w_gate, w_up, w_down = (
        lax.all_to_all(w, "ep", split_axis=0, concat_axis=1, tiled=True)[0]
        for w in reorder(inverse, gate_old, up_old, down_old)
    )
    named = routing[:, :, None] == expert_ids[None, None, :]
    hits = jnp.any(named, axis=1)
    order = jnp.arange(tok_count, dtype=jnp.int32)
    below = (order[:, None] > order[None, :]).astype(jnp.bfloat16)
    rank = jnp.dot(below, hits.astype(jnp.bfloat16), preferred_element_type=jnp.float32)
    place = jnp.where(hits, rank, -1.0).astype(jnp.int32)
    ranks = jnp.arange(CAP, dtype=jnp.int32)
    pick = (place.T[:, None, :] == ranks[None, :, None]).astype(jnp.bfloat16)
    pick = pick.reshape(expert_total * CAP, tok_count)
    gate_of = jnp.sum(jnp.where(named, gates.astype(jnp.float32)[:, :, None], 0.0), axis=1)
    gate_send = jnp.sum(
        pick.reshape(expert_total, CAP, tok_count).astype(jnp.float32) * gate_of.T[:, None, :],
        axis=2,
    ).reshape(-1)
    both = jnp.concatenate([tokens, cotangent], axis=1)
    rows_send = jnp.dot(pick, both, preferred_element_type=jnp.float32).astype(jnp.bfloat16)
    rows_quarter = lax.all_to_all(rows_send, "ep", split_axis=0, concat_axis=0, tiled=True)
    weight_g = lax.all_to_all(gate_send, "ep", split_axis=0, concat_axis=0, tiled=True)[:, None]
    quarter = tokens.shape[1]
    rows_in = lax.all_gather(rows_quarter[:, :quarter], "th", axis=1, tiled=True)
    rows_grad = lax.all_gather(rows_quarter[:, quarter:], "th", axis=1, tiled=True)
    gate_pre = jnp.dot(rows_in, w_gate, preferred_element_type=jnp.float32)
    up_pre = jnp.dot(rows_in, w_up, preferred_element_type=jnp.float32)
    back_hid = jnp.dot(rows_grad, w_down, preferred_element_type=jnp.float32)
    sigmoid_gate = jax.nn.sigmoid(gate_pre)
    silu_gate = gate_pre * sigmoid_gate
    hidden = silu_gate * up_pre
    grad_hid = weight_g * back_hid
    grad_gate_pre = (
        grad_hid * up_pre * sigmoid_gate * (1.0 + gate_pre * (1.0 - sigmoid_gate))
    ).astype(jnp.bfloat16)
    grad_up_pre = (grad_hid * silu_gate).astype(jnp.bfloat16)
    scaled_hidden = (weight_g * hidden).astype(jnp.bfloat16)
    router_part = jnp.sum(back_hid * hidden, axis=1)
    over_rows = (((0,), (0,)), ((), ()))
    grad_wg, grad_wu, grad_wd = (
        lax.dot_general(a, b, over_rows, preferred_element_type=jnp.float32).astype(jnp.bfloat16)[
            None
        ]
        for a, b in (
            (rows_in, grad_gate_pre),
            (rows_in, grad_up_pre),
            (rows_grad, scaled_hidden),
        )
    )
    over_hidden = (((1,), (1,)), ((), ()))
    partial_value = lax.dot_general(
        grad_gate_pre, w_gate, over_hidden, preferred_element_type=jnp.float32
    ) + lax.dot_general(grad_up_pre, w_up, over_hidden, preferred_element_type=jnp.float32)
    slot_grad = lax.psum_scatter(
        partial_value.astype(jnp.bfloat16), "th", scatter_dimension=1, tiled=True
    )
    router_term = lax.psum(router_part, "th").astype(jnp.bfloat16)
    back_rows = lax.all_to_all(slot_grad, "ep", split_axis=0, concat_axis=0, tiled=True)
    back_router = lax.all_to_all(router_term, "ep", split_axis=0, concat_axis=0, tiled=True)
    grad_tokens = lax.dot_general(
        pick, back_rows, over_rows, preferred_element_type=jnp.float32
    ).astype(jnp.bfloat16)
    router_of = jnp.sum(
        (pick.astype(jnp.float32) * back_router.astype(jnp.float32)[:, None]).reshape(
            expert_total, CAP, tok_count
        ),
        axis=1,
    ).T
    grad_gates = jnp.sum(jnp.where(named, router_of[:, None, :], 0.0), axis=2)
    return (grad_tokens, grad_gates.astype(jnp.bfloat16), grad_wg, grad_wu, grad_wd)


def solution(mesh):
    placed = (
        P("ep", "th"),
        P("ep", "th"),
        P("ep", None),
        P("ep", None),
        P(),
        P(None, "ep", "th"),
        P(None, "ep", "th"),
        P(None, "ep", "th"),
    )
    return jax.shard_map(
        local,
        mesh=mesh,
        in_specs=placed,
        out_specs=(
            P("ep", "th"),
            P("ep", None),
            P("ep", None, "th"),
            P("ep", None, "th"),
            P("ep", None, "th"),
        ),
        check_vma=False,
    )
```

time: 740 us -> 508 us (0.69)
  local copies, waits for them, and re-layouts: 124 us -> 25.7 us
  blocking collectives: 187 us -> 132 us
  starting transfers between devices: 65.8 us -> 27.8 us
  waiting for transfers between devices: 220 us -> 185 us
  other arithmetic: 36.4 us -> 6.6 us
  Pallas kernels: 0 us -> 21.1 us
    all_to_all x4 -> x2, waiting for transfers between devices: 161 us -> 63 us  [local(): lax.all_to_all(w, 'ep', split_axis=0, concat_axis=1, tiled=True)[0]]
    gather x10 -> x0, local copies, waits for them, and re-layouts: 98 us -> none  [the longest x2 32.9 us: local(): full_cot[token_index] * live]
    all_to_all x2 -> x3, blocking collectives: 172 us -> 125 us  [the longest x1 70.5 us: local(): lax.all_to_all(rows_send, 'ep', split_axis=0, concat_axis=0, tiled=True)]
    all_gather x2, waiting for transfers between devices: 0.02 us -> 30.2 us  [the longest x1 30.2 us: local(): lax.all_gather(rows_quarter[:, quarter:], 'th', axis=1, tiled=True)]
    reduce_scatter x1, waiting for transfers between devices: 42.3 us -> 72.4 us  [local(): lax.psum_scatter(partial_value.astype(jnp.bfloat16), 'th', scatter_dimens...]
    all_to_all x1, starting transfers between devices: 34.6 us -> 9.71 us  [local(): lax.all_to_all(router_term, 'ep', split_axis=0, concat_axis=0, tiled=True)]
    pallas_call x0 -> x1, Pallas kernels: none -> 21.1 us  [reorder(): pl.pallas_call(reorder_body, out_shape=[jax.ShapeDtypeStruct(gate_old.sha...]
    mul x3 -> x0, other arithmetic: 15.9 us -> none  [the longest x1 15.9 us: local(): full_cot[token_index] * live]
  transfers between devices with their start and end apart: 9 -> 7, of which waited for: 4 -> 6; matrix products, arithmetic and copies ran while one was open for 21% -> 10% of each run, Pallas kernels for 0% -> 4%
where the time goes in v1:
time: 508 us; the launch traced here: 502 us
  waiting for transfers between devices  185 us (36%)
  blocking collectives  132 us (26%)
  matrix products  90.2 us (18%)
  starting transfers between devices  27.8 us (5%)
  local copies, waits for them, and re-layouts  25.7 us (5%)
  Pallas kernels  21.1 us (4%)
  between operations  14.2 us (3%)
  other arithmetic  6.6 us (1%)
    reduce_scatter x1, waiting for transfers between devices, local(): lax.psum_scatter(partial_value.astype(jnp.bfloat16), 'th', scatter_dimens...  72.4 us
    all_to_all x1, blocking collectives, local(): lax.all_to_all(rows_send, 'ep', split_axis=0, concat_axis=0, tiled=True)  70.5 us
    all_to_all x2, waiting for transfers between devices, local(): lax.all_to_all(w, 'ep', split_axis=0, concat_axis=1, tiled=True)[0]  63 us
    all_to_all x1, blocking collectives, local(): lax.all_to_all(w, 'ep', split_axis=0, concat_axis=1, tiled=True)[0]  43.3 us
    dot_general x3, matrix products, local(): lax.dot_general(a, b, over_rows, preferred_element_type=jnp.float32)  33.5 us
    all_gather x1, waiting for transfers between devices, local(): lax.all_gather(rows_quarter[:, quarter:], 'th', axis=1, tiled=True)  30.2 us
    pallas_call x1, Pallas kernels, reorder(): pl.pallas_call(reorder_body, out_shape=[jax.ShapeDtypeStruct(gate_old.sha...  21.1 us
    all_to_all x2, local copies, waits for them, and re-layouts, local(): lax.all_to_all(rows_send, 'ep', split_axis=0, concat_axis=0, tiled=True)  14.5 us
  transfers between devices with their start and end apart: 7, of which 6 were waited for; matrix products, arithmetic and copies ran while one was open for 10% of the time, Pallas kernels for 4%

profile of v1, /device:TPU:1, one launch (start us, length us, event | category | flops | bytes accessed | tf_op | source)
XLA Modules:
  0.0 502.1 jit_solution(14792340210063658070)
XLA Ops:
  7.2 0.0 all-gather.5.cloned.1.call-start
  7.2 0.7 fusion.17
  7.9 0.1 fusion.5
  8.1 0.1 eq.60
  8.3 4.7 convolution_convert_fusion
  13.0 7.2 %all_to_all.49 = bf16[32,36,2048]{2,1,0:T(8,128)(2,1)} reshape(bf16[1152,2048]{1,0:T(8,128)(2,1)} %convolution_convert_fusion) | data formatting | bytes 9437184 | tf_op jit(solution)/shard_map/all_to_all | solution.py:58
  20.2 70.5 %all_to_all.67 = bf16[32,36,2048]{2,1,0:T(8,128)(2,1)} all-to-all(bf16[32,36,2048]{2,1,0:T(8,128)(2,1)} %all_to_all.49), channel_id=1, replica_groups=mesh['ep'=32,'th'=4] {'ep'}, dimensions={0} | all-to-all | bytes 9437184 | tf_op jit(solution)/shard_map/all_to_all | solution.py:58
  90.7 7.3 %all_to_all.51 = bf16[1152,2048]{1,0:T(8,128)(2,1)} reshape(bf16[32,36,2048]{2,1,0:T(8,128)(2,1)} %all_to_all.67) | data formatting | bytes 9437184 | tf_op jit(solution)/shard_map/all_to_all | solution.py:58
  98.0 5.1 %fusion.20 = (bf16[1152,1024]{1,0:T(8,128)(2,1)}, bf16[1152,1024]{1,0:T(8,128)(2,1)}) fusion(bf16[1152,2048]{1,0:T(8,128)(2,1)} %all_to_all.51), kind=kLoop, calls=%fused_computation.40 | loop fusion | bytes 9437184 | tf_op jit(solution)/shard_map/slice | solution.py:62
  103.1 0.0 all-gather.5.cloned.1.call-update
  103.1 0.0 all-gather.3.cloned.1.call-start
  103.1 0.7 all-gather.3.cloned.1.call-update
  103.8 0.6 select_reduce_fusion.2.inverse
  104.5 21.1 %shard_map.119 = (bf16[32,128,384]{2,1,0:T(8,128)(2,1)}, bf16[32,128,384]{2,1,0:T(8,128)(2,1)}, bf16[32,128,384]{2,1,0:T(8,128)(2,1)}) custom-call(s32[32]{0:T(128)} %select_reduce_fusion.2.inverse, bf16[32,128,384]{2,1,0:T(8,128)(2,1)} %gate_ref.1, bf16[32,128,384]{2,1,0:T(8,128)(2,1)} %up_ref.1, bf16[32,128,384]{2,1,0:T(8,128)(2,1)} %down_ref.1), custom_call_target="tpu_custom_call" | custom-call | tf_op jit(solution)/shard_map/pallas_call | solution.py:22
  125.5 43.3 %all_to_all.68 = bf16[32,128,384]{2,1,0:T(8,128)(2,1)S(1)} all-to-all(bf16[32,128,384]{2,1,0:T(8,128)(2,1)} %get-tuple-element.9), channel_id=1, replica_groups=mesh['ep'=32,'th'=4] {'ep'}, dimensions={0} | all-to-all | bytes 6291456 | tf_op jit(solution)/shard_map/all_to_all | solution.py:39
  168.9 4.7 all-to-all-start.4
  173.7 39.9 %all-to-all-done.4 = bf16[32,128,384]{2,1,0:T(8,128)(2,1)} async-done(((bf16[32,128,384]{2,1,0:T(8,128)(2,1)}), bf16[32,128,384]{2,1,0:T(8,128)(2,1)}, u32[]{:S(2)}, u32[]{:S(2)}) %all-to-all-start.4) | async-done | bytes 3145760 | tf_op jit(solution)/shard_map/all_to_all | solution.py:39
  213.5 5.4 %all-to-all-start.2 = ((bf16[32,128,384]{2,1,0:T(8,128)(2,1)}), bf16[32,128,384]{2,1,0:T(8,128)(2,1)}, u32[]{:S(2)}, u32[]{:S(2)}) async-start(bf16[32,128,384]{2,1,0:T(8,128)(2,1)} %get-tuple-element.8), calls=%async_computation.2 | async-start | bytes 6291456 | tf_op jit(solution)/shard_map/all_to_all | solution.py:39
  218.9 0.0 all-gather.5.cloned.1.call-done
  219.0 10.4 %fusion.22 = f32[1152,384]{0,1:T(8,128)} fusion(bf16[1152,4096]{1,0:T(8,128)(2,1)} %all-gather.5.cloned.1.call-done, bf16[4096,384]{1,0:T(8,128)(2,1)} %bitcast.5), kind=kOutput, calls=%fused_computation.42 | convolution fusion | flops 3623878656 | bytes 14352384 | tf_op jit(solution)/shard_map/dot_general | solution.py:63
  229.4 5.8 %fusion.21 = f32[1152,384]{0,1:T(8,128)} fusion(bf16[1152,4096]{1,0:T(8,128)(2,1)S(1)} %copy-done.8, bf16[4096,384]{1,0:T(8,128)(2,1)S(1)} %bitcast.37), kind=kOutput, calls=%fused_computation.41 | convolution fusion | flops 3623878656 | bytes 14352384 | tf_op jit(solution)/shard_map/dot_general | solution.py:64
  235.3 23.1 %all-to-all-done.2 = bf16[32,128,384]{2,1,0:T(8,128)(2,1)} async-done(((bf16[32,128,384]{2,1,0:T(8,128)(2,1)}), bf16[32,128,384]{2,1,0:T(8,128)(2,1)}, u32[]{:S(2)}, u32[]{:S(2)}) %all-to-all-start.2) | async-done | bytes 3145760 | tf_op jit(solution)/shard_map/all_to_all | solution.py:39
  258.4 30.2 %all-gather.3.cloned.1.call-done = bf16[1152,4096]{1,0:T(8,128)(2,1)} async-done(((bf16[1152,1024]{1,0:T(8,128)(2,1)}), bf16[1152,4096]{1,0:T(8,128)(2,1)}) %all-gather.3.cloned.1.call-update) | async-done | bytes 9437200 | tf_op jit(solution)/shard_map/all_gather | solution.py:62
  288.6 11.5 %multiply_reduce_fusion = (f32[1152]{0:T(1024)S(1)}, f32[1152,384]{0,1:T(8,128)}) fusion(f32[1152,384]{0,1:T(8,128)} %fusion.21, f32[1152,384]{0,1:T(8,128)} %fusion.22, bf16[1152,4096]{1,0:T(8,128)(2,1)} %all-gather.3.cloned.1.call-done, bf16[4096,384]{1,0:T(8,128)(2,1)} %bitcast.3), kind=kOutput, calls=%fused_computation.9 | convolution fusion | flops 3626974208 | bytes 17895936 | tf_op jit(solution)/shard_map/dot_general | solution.py:65
  300.0 7.3 %psum.7 = bf16[1152]{0:T(1024)(128)(2,1)S(1)} all-reduce(f32[1152]{0:T(1024)S(1)} %get-tuple-element.17), channel_id=1, replica_groups=mesh['ep'=32,'th'=4] {'th'}, use_global_device_ids=true, to_apply=%region_6.7 | all-reduce | flops 1152 | bytes 6912 | tf_op jit(solution)/shard_map/psum | solution.py:94
  307.4 0.7 all_to_all.59
  308.1 9.7 %all-to-all-start.6 = ((bf16[32,36,1]{1,2,0:T(2,128)(2,1)}), bf16[32,36,1]{1,2,0:T(2,128)(2,1)S(1)}, u32[]{:S(2)}, u32[]{:S(2)}) async-start(bf16[32,36,1]{1,2,0:T(2,128)(2,1)} %all_to_all.59), calls=%async_computation.7 | async-start | bytes 32768 | tf_op jit(solution)/shard_map/all_to_all | solution.py:96
  317.8 0.0 reduce-scatter.2.cloned.1.call-start
  317.9 6.8 %all-to-all-done.6 = bf16[32,36,1]{1,2,0:T(2,128)(2,1)S(1)} async-done(((bf16[32,36,1]{1,2,0:T(2,128)(2,1)}), bf16[32,36,1]{1,2,0:T(2,128)(2,1)S(1)}, u32[]{:S(2)}, u32[]{:S(2)}) %all-to-all-start.6) | async-done | bytes 2336 | tf_op jit(solution)/shard_map/all_to_all | solution.py:96
  324.7 0.5 fusion.9
  325.2 10.7 %all_to_all.69 = f32[32,36,1]{1,2,0:T(1,128)S(1)} all-to-all(f32[32,36,1]{1,2,0:T(1,128)S(1)} %bitcast.42), channel_id=1, replica_groups=mesh['ep'=32,'th'=4] {'ep'}, dimensions={0} | all-to-all | bytes 9216 | tf_op jit(solution)/shard_map/all_to_all | solution.py:59
  335.9 0.5 broadcast.39
  336.4 0.7 reduce.3
  337.1 0.1 mul.67
  337.2 3.4 multiply_convert_fusion.1
  340.7 11.5 %fusion.23 = f32[1152,4096]{1,0:T(8,128)} fusion(bf16[1152,384]{0,1:T(8,128)(2,1)S(1)} %get-tuple-element.16, bf16[4096,384]{1,0:T(8,128)(2,1)} %bitcast.5), kind=kOutput, calls=%fused_computation.43 | convolution fusion | flops 3623878656 | bytes 22904832 | tf_op jit(solution)/shard_map/dot_general | solution.py:88
  352.1 11.4 %add_convert_fusion = bf16[1152,4096]{1,0:T(8,128)(2,1)} fusion(f32[1152,4096]{1,0:T(8,128)} %fusion.23, bf16[1152,384]{0,1:T(8,128)(2,1)S(1)} %get-tuple-element.15, bf16[4096,384]{1,0:T(8,128)(2,1)S(1)} %bitcast.38), kind=kOutput, calls=%fused_computation | convolution fusion | flops 3633315840 | bytes 32342016 | tf_op jit(solution)/shard_map/dot_general | solution.py:90
  363.5 0.0 reduce-scatter.2.cloned.1.call-update
  363.5 0.6 select_reduce_fusion
  364.1 0.5 copy-done.1
  364.7 11.2 %fusion.1 = bf16[1,4096,384]{2,1,0:T(8,128)(2,1)} fusion(bf16[1152,4096]{1,0:T(8,128)(2,1)} %all-gather.5.cloned.1.call-done, bf16[1152,384]{0,1:T(8,128)(2,1)S(1)} %copy-done.1), kind=kOutput, calls=%fused_computation.6 | convolution fusion | flops 3625451520 | bytes 13467648 | tf_op jit(solution)/shard_map/dot_general | solution.py:78
  375.9 72.4 %reduce-scatter.2.cloned.1.call-done = bf16[1152,1024]{1,0:T(8,128)(2,1)} async-done(((bf16[1152,4096]{1,0:T(8,128)(2,1)}), bf16[1152,1024]{1,0:T(8,128)(2,1)}) %reduce-scatter.2.cloned.1.call-update) | async-done | bytes 2359312 | tf_op jit(solution)/shard_map/reduce_scatter | solution.py:91
  448.3 4.1 all_to_all.55
  452.4 7.8 %all-to-all-start.5 = ((bf16[32,36,1024]{2,1,0:T(8,128)(2,1)}), bf16[32,36,1024]{2,1,0:T(8,128)(2,1)S(1)}, u32[]{:S(2)}, u32[]{:S(2)}) async-start(bf16[32,36,1024]{2,1,0:T(8,128)(2,1)} %all_to_all.55), calls=%async_computation.6 | async-start | bytes 5242880 | tf_op jit(solution)/shard_map/all_to_all | solution.py:95
  460.2 11.1 %fusion = bf16[1,4096,384]{2,1,0:T(8,128)(2,1)} fusion(bf16[1152,4096]{1,0:T(8,128)(2,1)} %all-gather.5.cloned.1.call-done, bf16[1152,384]{0,1:T(8,128)(2,1)S(1)} %copy-done.3), kind=kOutput, calls=%fused_computation.5 | convolution fusion | flops 3625451520 | bytes 13467648 | tf_op jit(solution)/shard_map/dot_general | solution.py:78
  471.3 11.2 %fusion.2 = bf16[1,4096,384]{2,1,0:T(8,128)(2,1)} fusion(bf16[1152,4096]{1,0:T(8,128)(2,1)} %all-gather.3.cloned.1.call-done, f32[1152]{0:T(1024)S(1)} %mul.67, f32[1152,384]{0,1:T(8,128)S(1)} %copy-done.5, f32[1152,384]{0,1:T(8,128)S(1)} %copy-done.4), kind=kOutput, calls=%fused_computation.7 | convolution fusion | flops 3628548096 | bytes 16126464 | tf_op jit(solution)/shard_map/dot_general | solution.py:78
  482.5 11.6 %all-to-all-done.5 = bf16[32,36,1024]{2,1,0:T(8,128)(2,1)S(1)} async-done(((bf16[32,36,1024]{2,1,0:T(8,128)(2,1)}), bf16[32,36,1024]{2,1,0:T(8,128)(2,1)S(1)}, u32[]{:S(2)}, u32[]{:S(2)}) %all-to-all-start.5) | async-done | bytes 2359328 | tf_op jit(solution)/shard_map/all_to_all | solution.py:95
  494.1 1.3 fusion.4
  (25 shorter events, 0.2 us)
Async XLA Ops:
  7.2 211.8 %all-gather.5.cloned.1.call-start = ((), (), s32[]{:S(2)}) async-start(), calls=%async_computation.9 | async-start | bytes 11796480 | tf_op jit(solution)/shard_map/all_gather | solution.py:61
  103.1 0.8 copy-start.9
  103.1 185.5 %all-gather.3.cloned.1.call-start = ((), (), s32[]{:S(2)}) async-start(), calls=%async_computation.8 | async-start | bytes 11796480 | tf_op jit(solution)/shard_map/all_gather | solution.py:62
  168.9 4.8 copy-start.7
  168.9 44.6 %all-to-all-start.4 = ((bf16[32,128,384]{2,1,0:T(8,128)(2,1)}), bf16[32,128,384]{2,1,0:T(8,128)(2,1)}, u32[]{:S(2)}, u32[]{:S(2)}) async-start(bf16[32,128,384]{2,1,0:T(8,128)(2,1)} %get-tuple-element.10), calls=%async_computation.4 | async-start | bytes 6291456 | tf_op jit(solution)/shard_map/all_to_all | solution.py:39
  213.5 44.8 %all-to-all-start.2 = ((bf16[32,128,384]{2,1,0:T(8,128)(2,1)}), bf16[32,128,384]{2,1,0:T(8,128)(2,1)}, u32[]{:S(2)}, u32[]{:S(2)}) async-start(bf16[32,128,384]{2,1,0:T(8,128)(2,1)} %get-tuple-element.8), calls=%async_computation.2 | async-start | bytes 6291456 | tf_op jit(solution)/shard_map/all_to_all | solution.py:39
  219.0 10.4 %copy-start.8 = (bf16[1152,4096]{1,0:T(8,128)(2,1)S(1)}, bf16[1152,4096]{1,0:T(8,128)(2,1)}, u32[]{:S(2)}) copy-start(bf16[1152,4096]{1,0:T(8,128)(2,1)} %all-gather.5.cloned.1.call-done) | copy-start | bytes 28311556
  288.6 29.3 %copy-start.6 = (s32[128,8]{0,1:T(8,128)S(1)}, s32[128,8]{0,1:T(8,128)}, u32[]{:S(2)}) copy-start(s32[128,8]{0,1:T(8,128)} %param.11) | copy-start | bytes 12292
  308.1 16.6 %all-to-all-start.6 = ((bf16[32,36,1]{1,2,0:T(2,128)(2,1)}), bf16[32,36,1]{1,2,0:T(2,128)(2,1)S(1)}, u32[]{:S(2)}, u32[]{:S(2)}) async-start(bf16[32,36,1]{1,2,0:T(2,128)(2,1)} %all_to_all.59), calls=%async_computation.7 | async-start | bytes 32768 | tf_op jit(solution)/shard_map/all_to_all | solution.py:96
  317.8 130.5 %reduce-scatter.2.cloned.1.call-start = ((), (), s32[]{:S(2)}) async-start(), calls=%async_computation.10 | async-start | bytes 11796480 | tf_op jit(solution)/shard_map/reduce_scatter | solution.py:91
  340.6 11.5 %copy-start.2 = (bf16[1152,384]{0,1:T(8,128)(2,1)}, bf16[1152,384]{0,1:T(8,128)(2,1)S(1)}, u32[]{:S(2)}) copy-start(bf16[1152,384]{0,1:T(8,128)(2,1)S(1)} %get-tuple-element.16) | copy-start | bytes 2654212
  340.6 11.5 %copy-start = (bf16[1152,384]{0,1:T(8,128)(2,1)}, bf16[1152,384]{0,1:T(8,128)(2,1)S(1)}, u32[]{:S(2)}) copy-start(bf16[1152,384]{0,1:T(8,128)(2,1)S(1)} %get-tuple-element.15) | copy-start | bytes 2654212
  363.5 1.2 copy-start.1
  452.4 7.8 %copy-start.3 = (bf16[1152,384]{0,1:T(8,128)(2,1)S(1)}, bf16[1152,384]{0,1:T(8,128)(2,1)}, u32[]{:S(2)}) copy-start(bf16[1152,384]{0,1:T(8,128)(2,1)} %copy-done.2) | copy-start | bytes 2654212
  452.4 41.7 %all-to-all-start.5 = ((bf16[32,36,1024]{2,1,0:T(8,128)(2,1)}), bf16[32,36,1024]{2,1,0:T(8,128)(2,1)S(1)}, u32[]{:S(2)}, u32[]{:S(2)}) async-start(bf16[32,36,1024]{2,1,0:T(8,128)(2,1)} %all_to_all.55), calls=%async_computation.6 | async-start | bytes 5242880 | tf_op jit(solution)/shard_map/all_to_all | solution.py:95
  460.2 11.1 %copy-start.4 = (f32[1152,384]{0,1:T(8,128)S(1)}, f32[1152,384]{0,1:T(8,128)}, u32[]{:S(2)}) copy-start(f32[1152,384]{0,1:T(8,128)} %fusion.22) | copy-start | bytes 5308420
  460.2 11.1 %copy-start.5 = (f32[1152,384]{0,1:T(8,128)S(1)}, f32[1152,384]{0,1:T(8,128)}, u32[]{:S(2)}) copy-start(f32[1152,384]{0,1:T(8,128)} %fusion.21) | copy-start | bytes 5308420
Sparse Core Ops, SparseCore 0:
  103.2 90.5 all-gather.4
  195.5 93.0 all-gather.2
  363.6 84.6 reduce-scatter.1

commit v2 on v1

v2 whole, which is shorter than its diff:
```python
import jax
import jax.numpy as jnp
from jax import lax
from jax.experimental import pallas as pl
from jax.experimental.pallas import tpu as pltpu
from jax.sharding import PartitionSpec as P

CAP = 36
PEERS = 32
SET = 4
CHUNKS = 4
SETS = PEERS // SET
PER = SETS // CHUNKS
SROWS = SET * CAP
CROWS = PER * SROWS
MESH = pl.DeviceIdType.MESH
F32 = jnp.float32
BF16 = jnp.bfloat16


def offset(k):
    m = k // 2
    return m % 4, (m // 4 + m % 4) % 4, k % 2


def peer_to(me, k):
    dx, dy, dc = offset(k)
    return (me // 8 + dx) % 4 * 8 + ((me // 2) % 4 + dy) % 4 * 2 + (me % 2 + dc) % 2


def peer_from(me, k):
    dx, dy, dc = offset(k)
    return (me // 8 + 4 - dx) % 4 * 8 + ((me // 2) % 4 + 4 - dy) % 4 * 2 + (me % 2 + dc) % 2


def reorder_body(order, gate_ref, up_ref, down_ref, out_ref, held, in_sems, out_sems):
    depth = gate_ref.shape[1]

    def reads(k):
        return [
            pltpu.make_async_copy(
                ref.at[order[k]], held.at[k, pl.ds(n * depth, depth)], in_sems.at[n, k]
            )
            for n, ref in enumerate((gate_ref, up_ref, down_ref))
        ]

    def write(k):
        return pltpu.make_async_copy(held.at[k], out_ref.at[k], out_sems.at[k])

    @pl.loop(0, PEERS)
    def _(k):
        for copy in reads(k):
            copy.start()

    @pl.loop(0, PEERS)
    def _(k):
        for copy in reads(k):
            copy.wait()
        write(k).start()

    @pl.loop(0, PEERS)
    def _(k):
        write(k).wait()


def reorder(order, gate_old, up_old, down_old):
    count, depth, cols = gate_old.shape
    return pl.pallas_call(
        reorder_body,
        out_shape=jax.ShapeDtypeStruct((count, 3 * depth, cols), gate_old.dtype),
        grid_spec=pltpu.PrefetchScalarGridSpec(
            num_scalar_prefetch=1,
            grid=(),
            in_specs=[pl.BlockSpec(memory_space=pl.ANY)] * 3,
            out_specs=pl.BlockSpec(memory_space=pl.ANY),
            scratch_shapes=[
                pltpu.VMEM((count, 3 * depth, cols), gate_old.dtype),
                pltpu.SemaphoreType.DMA((3, count)),
                pltpu.SemaphoreType.DMA((count,)),
            ],
        ),
        compiler_params=pltpu.CompilerParams(vmem_limit_bytes=24 * 2**20),
    )(order, gate_old, up_old, down_old)


def layer_body(
    rows_ref, gsend_ref, wsend_ref, pack_ref, packt_ref,
    gw_ref, back_ref, qback_ref,
    wv, xy, rr, gr, dab, acc, s1s, s1r, s2s, s2r, own, ret, qp, qr, qs, stage,
    row_s, row_r, g_s, g_r, w_s, w_r, z_s, z_r, v_s, v_r, s1_s, s1_r, s2_s, s2_r,
    b_s, b_r, q_s, q_r, qb_s, qb_r, o_s,
):
    me = lax.axis_index("ep")
    th = lax.axis_index("th")
    right, left, opp = (th + 1) % 4, (th + 3) % 4, (th + 2) % 4
    cols = wv.shape[2]

    def ep_copy(src, dst, s, r, p):
        return pltpu.make_async_remote_copy(
            src_ref=src, dst_ref=dst, send_sem=s, recv_sem=r, device_id={"ep": p},
            device_id_type=MESH,
        )

    def th_copy(src, dst, s, r, p):
        return pltpu.make_async_remote_copy(
            src_ref=src, dst_ref=dst, send_sem=s, recv_sem=r, device_id={"th": p},
            device_id_type=MESH,
        )

    barrier = pltpu.get_barrier_semaphore()

    @pl.loop(1, PEERS)
    def _(k):
        pl.semaphore_signal(
            barrier, inc=1, device_id={"ep": peer_to(me, k)}, device_id_type=MESH
        )

    for p in (right, left, opp):
        pl.semaphore_signal(barrier, inc=1, device_id={"th": p}, device_id_type=MESH)
    pl.semaphore_wait(barrier, PEERS - 1 + 3)

    def row_copy(k):
        return ep_copy(rows_ref.at[k], rr.at[k], row_s.at[k], row_r.at[k], peer_to(me, k))

    def g_copy(k):
        return ep_copy(gsend_ref.at[k], gr.at[k], g_s.at[k], g_r.at[k], peer_to(me, k))

    def w_copy(k):
        return ep_copy(wsend_ref.at[k], wv.at[me], w_s.at[k], w_r.at[k], peer_to(me, k))

    def w_wait(k):
        s = peer_from(me, k)
        ep_copy(wsend_ref.at[k], wv.at[s], w_s.at[k], w_r.at[k], s).wait_recv()

    row_own = pltpu.make_async_copy(rows_ref.at[0], rr.at[0], row_r.at[0])
    g_own = pltpu.make_async_copy(gsend_ref.at[0], gr.at[0], g_r.at[0])
    w_own = pltpu.make_async_copy(wsend_ref.at[0], wv.at[me], w_r.at[0])
    row_own.start()
    g_own.start()

    @pl.loop(1, PEERS)
    def _(k):
        g_copy(k).start()
        row_copy(k).start()

    w_own.start()

    @pl.loop(1, PEERS)
    def _(k):
        w_copy(k).start()

    def z_copies(i):
        return (
            th_copy(xy.at[th, i], xy.at[th, i], z_s.at[0, i], z_r.at[0, i], right),
            th_copy(xy.at[th, i], xy.at[th, i], z_s.at[1, i], z_r.at[1, i], left),
        )

    def z_wait(i):
        th_copy(xy.at[left, i], xy.at[left, i], z_s.at[0, i], z_r.at[0, i], left).wait_recv()
        th_copy(xy.at[right, i], xy.at[right, i], z_s.at[1, i], z_r.at[1, i], right).wait_recv()

    def v_copies(i):
        return (
            th_copy(xy.at[left, i, 0], xy.at[left, i, 0], v_s.at[0, i], v_r.at[0, i], right),
            th_copy(xy.at[right, i, 1], xy.at[right, i, 1], v_s.at[1, i], v_r.at[1, i], left),
        )

    def v_wait(i):
        th_copy(xy.at[opp, i, 0], xy.at[opp, i, 0], v_s.at[0, i], v_r.at[0, i], left).wait_recv()
        th_copy(xy.at[opp, i, 1], xy.at[opp, i, 1], v_s.at[1, i], v_r.at[1, i], right).wait_recv()

    def relay(i):
        z_wait(i)
        for copy in v_copies(i):
            copy.start()

    row_own.wait()
    g_own.wait()

    @pl.loop(0, CHUNKS)
    def _(i):
        for part in range(PER):
            base = (i * PER + part) * SET
            for n in range(SET):
                k = base + n

                @pl.when(k > 0)
                def _():
                    row_copy(k).wait_recv()
                    g_copy(k).wait_recv()

            arrived = rr[pl.ds(base, SET)].reshape(SET * SROWS, rr.shape[2])
            wide = rr.shape[2]
            for c in range(4):
                piece = jnp.dot(pack_ref[c], arrived, preferred_element_type=F32).astype(BF16)
                xy[th, i, c // 2, pl.ds(part * SROWS, SROWS), pl.ds(c % 2 * wide, wide)] = piece
        for copy in z_copies(i):
            copy.start()

        @pl.when(i > 0)
        def _():
            relay(i - 1)

    relay(CHUNKS - 1)

    w_own.wait()

    @pl.loop(1, PEERS)
    def _(k):
        w_wait(k)

    quarter = xy.shape[4]
    half = quarter // 2
    blocks = quarter // 128

    def weight(n, first, count):
        return wv[pl.ds(first, count), pl.ds(n * 128, 128), :].reshape(count * 128, cols)

    over_last = (((1,), (1,)), ((), ()))

    def partial(i, j, h):
        da, db = dab[0, i], dab[1, i]
        first = j * blocks + h * (blocks // 2)
        value = lax.dot_general(
            da, weight(0, first, blocks // 2), over_last, preferred_element_type=F32
        ) + lax.dot_general(
            db, weight(1, first, blocks // 2), over_last, preferred_element_type=F32
        )
        return value.astype(BF16)

    row_at = lax.broadcasted_iota(jnp.int32, (SROWS, 128), 0)
    lane_at = lax.broadcasted_iota(jnp.int32, (SROWS, 128), 1)
    source_at = (
        (row_at >= CAP).astype(jnp.int32)
        + (row_at >= 2 * CAP).astype(jnp.int32)
        + (row_at >= 3 * CAP).astype(jnp.int32)
    )
    in_place = lane_at == row_at - source_at * CAP

    def s1_copies(i):
        return (
            th_copy(s1s.at[i, 0], s1r.at[i, 0], s1_s.at[0, i], s1_r.at[0, i], right),
            th_copy(s1s.at[i, 1], s1r.at[i, 1], s1_s.at[1, i], s1_r.at[1, i], left),
        )

    def s2_copies(i):
        return (
            th_copy(s2s.at[i, 0], s2r.at[i, 0], s2_s.at[0, i], s2_r.at[0, i], right),
            th_copy(s2s.at[i, 1], s2r.at[i, 1], s2_s.at[1, i], s2_r.at[1, i], left),
        )

    def b_copy(k):
        return ep_copy(ret.at[k], back_ref.at[k], b_s.at[k], b_r.at[k], peer_from(me, k))

    b_own = pltpu.make_async_copy(ret.at[0], back_ref.at[0], b_r.at[0])

    def combine(i):
        for n, copy in enumerate(s1_copies(i)):
            copy.wait_recv()
            at = pl.ds(n * half, half)
            s2s[i, n, :, at] = (s2s[i, n, :, at].astype(F32) + s1r[i, n].astype(F32)).astype(BF16)
        for copy in s2_copies(i):
            copy.start()

    def finish(i):
        for copy in s2_copies(i):
            copy.wait_recv()
        strip = quarter // 4
        for part in range(PER):
            base = (i * PER + part) * SET
            at = pl.ds(part * SROWS, SROWS)
            packed = jnp.zeros((SET * SROWS, strip), F32)
            for c in range(4):
                span = pl.ds(c * strip, strip)
                total = (
                    own[i, at, span].astype(F32)
                    + s2r[i, 0, at, span].astype(F32)
                    + s2r[i, 1, at, span].astype(F32)
                ).astype(BF16)
                packed += jnp.dot(packt_ref[c], total, preferred_element_type=F32)
            ret[pl.ds(base, SET)] = packed.astype(BF16).reshape(SET, SROWS, strip)
            for n in range(SET):
                k = base + n

                @pl.when(k > 0)
                def _():
                    b_copy(k).start()

                @pl.when(k == 0)
                def _():
                    b_own.start()

    qp[...] = jnp.zeros_like(qp)

    @pl.loop(0, CHUNKS)
    def _(i):
        v_wait(i)
        acc[...] = jnp.zeros_like(acc)

        @pl.loop(0, 4)
        def _(j):
            x, y = xy[j, i, 0], xy[j, i, 1]
            first = j * blocks
            acc[0] += jnp.dot(x, weight(0, first, blocks), preferred_element_type=F32)
            acc[1] += jnp.dot(x, weight(1, first, blocks), preferred_element_type=F32)
            acc[2] += jnp.dot(y, weight(2, first, blocks), preferred_element_type=F32)

        for part in range(PER):
            s = i * PER + part
            at = pl.ds(part * SROWS, SROWS)
            gate = jnp.zeros((SROWS, 128), F32)
            for n in range(SET):
                one = gr[s * SET + n].astype(F32)[0:1, :]
                gate = jnp.where(in_place & (source_at == n), one, gate)
            g = jnp.sum(gate, axis=1, keepdims=True)
            a, b, u = acc[0, at], acc[1, at], acc[2, at]
            sig = jax.nn.sigmoid(a)
            silu = a * sig
            hidden = silu * b
            dh = g * u
            dab[0, i, at] = (dh * b * sig * (1.0 + a * (1.0 - sig))).astype(BF16)
            dab[1, i, at] = (dh * silu).astype(BF16)
            dab[2, i, at] = (g * hidden).astype(BF16)
            q = jnp.sum(u * hidden, axis=1, keepdims=True)
            for n in range(SET):
                mine = jnp.where(in_place & (source_at == n), q, 0.0)
                qp[s, pl.ds(n, 1), :] = jnp.sum(mine, axis=0, keepdims=True)

        s1s[i, 0] = partial(i, opp, 0)
        s1s[i, 1] = partial(i, opp, 1)
        for copy in s1_copies(i):
            copy.start()

        @pl.loop(0, 2)
        def _(h):
            span = pl.ds(pl.multiple_of(h * half, half), half)
            s2s[i, 0, :, span] = partial(i, right, h)
            s2s[i, 1, :, span] = partial(i, left, h)
            own[i, :, span] = partial(i, th, h)

        @pl.when(i > 0)
        def _():
            combine(i - 1)

        @pl.when(i > 1)
        def _():
            finish(i - 2)

    combine(CHUNKS - 1)

    q_copies = tuple(
        th_copy(qp, qr.at[n], q_s.at[n], q_r.at[n], p) for n, p in enumerate((right, left, opp))
    )
    for copy in q_copies:
        copy.start()
    finish(CHUNKS - 2)

    over_rows = (((0,), (0,)), ((), ()))

    def out_copies(t):
        return tuple(
            pltpu.make_async_copy(
                stage.at[t % 2, n], gw_ref.at[n, pl.ds(t * half, half)], o_s.at[t % 2, n]
            )
            for n in range(3)
        )

    def weight_grads(t):
        @pl.when(t > 1)
        def _():
            for copy in out_copies(t - 2):
                copy.wait()

        span = pl.ds(pl.multiple_of(t % 2 * half, half), half)
        for n, kind in enumerate((0, 0, 1)):
            rows = xy[t // 2, :, kind, :, span].reshape(CHUNKS * CROWS, half)
            hid = dab[n].reshape(CHUNKS * CROWS, cols)
            stage[t % 2, n] = lax.dot_general(
                rows, hid, over_rows, preferred_element_type=F32
            ).astype(BF16)
        for copy in out_copies(t):
            copy.start()

    pl.loop(0, 4)(weight_grads)

    finish(CHUNKS - 1)
    for copy in q_copies:
        copy.wait_recv()

    def qb_copy(k):
        return ep_copy(qs.at[k], qback_ref.at[k], qb_s.at[k], qb_r.at[k], peer_from(me, k))

    qb_own = pltpu.make_async_copy(qs.at[0], qback_ref.at[0], qb_r.at[0])
    for s in range(SETS):
        total = qp[s] + qr[0, s] + qr[1, s] + qr[2, s]
        for n in range(SET):
            qs[s * SET + n] = jnp.broadcast_to(total[n : n + 1, :], (16, 128)).astype(BF16)
    qb_own.start()

    @pl.loop(1, PEERS)
    def _(k):
        qb_copy(k).start()

    pl.loop(4, 8)(weight_grads)
    for t in (6, 7):
        for copy in out_copies(t):
            copy.wait()

    qb_own.wait()
    b_own.wait()

    @pl.loop(1, PEERS)
    def _(k):
        row_copy(k).wait_send()
        g_copy(k).wait_send()
        w_copy(k).wait_send()
        b_copy(k).wait()
        qb_copy(k).wait()

    for copy in q_copies:
        copy.wait_send()

    @pl.loop(0, CHUNKS)
    def _(i):
        for copy in (*z_copies(i), *v_copies(i), *s1_copies(i), *s2_copies(i)):
            copy.wait_send()


def layer(rows_send, gate_send, w_send, pack, packt, width, quarter):
    cols = w_send.shape[2]
    wide = rows_send.shape[2]
    strip = quarter // 4
    half = quarter // 2
    dma = pltpu.SemaphoreType.DMA
    peer, ring = dma((PEERS,)), dma((2, CHUNKS))
    anywhere = pl.BlockSpec(memory_space=pl.ANY)
    inside = pl.BlockSpec(memory_space=pltpu.VMEM)
    return pl.pallas_call(
        layer_body,
        out_shape=[
            jax.ShapeDtypeStruct((3, width, cols), BF16),
            jax.ShapeDtypeStruct((PEERS, SROWS, strip), BF16),
            jax.ShapeDtypeStruct((PEERS, 16, 128), BF16),
        ],
        in_specs=[anywhere] * 3 + [inside] * 2,
        out_specs=[anywhere] * 3,
        scratch_shapes=[
            pltpu.VMEM((PEERS, 3 * 128, cols), BF16),
            pltpu.VMEM((4, CHUNKS, 2, CROWS, quarter), BF16),
            pltpu.VMEM((PEERS, SROWS, wide), BF16),
            pltpu.VMEM((PEERS, 16, 128), BF16),
            pltpu.VMEM((3, CHUNKS, CROWS, cols), BF16),
            pltpu.VMEM((3, CROWS, cols), F32),
            pltpu.VMEM((CHUNKS, 2, CROWS, half), BF16),
            pltpu.VMEM((CHUNKS, 2, CROWS, half), BF16),
            pltpu.VMEM((CHUNKS, 2, CROWS, quarter), BF16),
            pltpu.VMEM((CHUNKS, 2, CROWS, quarter), BF16),
            pltpu.VMEM((CHUNKS, CROWS, quarter), BF16),
            pltpu.VMEM((PEERS, SROWS, strip), BF16),
            pltpu.VMEM((SETS, 8, 128), F32),
            pltpu.VMEM((3, SETS, 8, 128), F32),
            pltpu.VMEM((PEERS, 16, 128), BF16),
            pltpu.VMEM((2, 3, half, cols), BF16),
            peer, peer, peer, peer, peer, peer,
            ring, ring, ring, ring, ring, ring, ring, ring,
            peer, peer, dma((3,)), dma((3,)), peer, peer, dma((2, 3)),
        ],
        compiler_params=pltpu.CompilerParams(
            collective_id=0, has_side_effects=True, vmem_limit_bytes=63 * 2**20
        ),
    )(rows_send, gate_send, w_send, pack, packt)


def local(tokens, cotangent, gates, routing, new_slot, gate_old, up_old, down_old):
    tok_count = routing.shape[0]
    quarter = tokens.shape[1]
    ids = jnp.arange(PEERS, dtype=jnp.int32)
    expert = peer_to(lax.axis_index("ep"), ids)
    order = jnp.sum(
        (new_slot[None, :] == expert[:, None]).astype(jnp.int32) * ids[None, :], axis=1
    )
    w_send = reorder(order, gate_old, up_old, down_old)
    named = routing[:, :, None] == expert[None, None, :]
    hits = jnp.any(named, axis=1)
    at = jnp.arange(tok_count, dtype=jnp.int32)
    below = (at[:, None] > at[None, :]).astype(BF16)
    rank = jnp.dot(below, hits.astype(BF16), preferred_element_type=F32)
    place = jnp.where(hits, rank, -1.0).astype(jnp.int32)
    ranks = jnp.arange(CAP, dtype=jnp.int32)
    pick = place.T[:, None, :] == ranks[None, :, None]
    group = jnp.arange(4, dtype=jnp.int32)
    spread = (
        pick[:, None, :, None, :] & (group[:, None] == group[None, :])[None, :, None, :, None]
    ).astype(BF16)
    spread = spread.reshape(PEERS * 4 * CAP, 4 * tok_count)
    both = jnp.concatenate([tokens, cotangent], axis=1)
    stacked = both.reshape(tok_count, 4, -1).transpose(1, 0, 2).reshape(4 * tok_count, -1)
    rows_send = jnp.dot(spread, stacked, preferred_element_type=F32).astype(BF16)
    gate_of = jnp.sum(jnp.where(named, gates.astype(F32)[:, :, None], 0.0), axis=1)
    gate_rows = jnp.sum(jnp.where(pick, gate_of.T[:, None, :], 0.0), axis=2)
    gate_send = jnp.broadcast_to(
        jnp.pad(gate_rows, ((0, 0), (0, 128 - CAP)))[:, None, :], (PEERS, 16, 128)
    ).astype(BF16)
    row = jnp.arange(SROWS, dtype=jnp.int32)
    from_row = (row // CAP * SROWS + row % CAP)[None, :] + group[:, None] * CAP
    spot = jnp.arange(SET * SROWS, dtype=jnp.int32)
    pack = (from_row[:, :, None] == spot[None, None, :]).astype(BF16)
    packt = (from_row[:, None, :] == spot[None, :, None]).astype(BF16)
    width = quarter * lax.axis_size("th")
    grads, back, qback = layer(
        rows_send.reshape(PEERS, SROWS, -1), gate_send, w_send, pack, packt, width, quarter
    )
    grad_stack = lax.dot_general(
        spread,
        back.reshape(PEERS * SROWS, -1),
        (((0,), (0,)), ((), ())),
        preferred_element_type=F32,
    ).astype(BF16)
    grad_tokens = (
        grad_stack.reshape(4, tok_count, -1).transpose(1, 0, 2).reshape(tok_count, quarter)
    )
    router = qback[:, 0, :CAP].astype(F32)
    router_of = jnp.sum(jnp.where(pick, router[:, :, None], 0.0), axis=1).T
    grad_gates = jnp.sum(jnp.where(named, router_of[:, None, :], 0.0), axis=2)
    return (grad_tokens, grad_gates.astype(BF16), grads[0:1], grads[1:2], grads[2:3])


def solution(mesh):
    placed = (
        P("ep", "th"),
        P("ep", "th"),
        P("ep", None),
        P("ep", None),
        P(),
        P(None, "ep", "th"),
        P(None, "ep", "th"),
        P(None, "ep", "th"),
    )
    return jax.shard_map(
        local,
        mesh=mesh,
        in_specs=placed,
        out_specs=(
            P("ep", "th"),
            P("ep", None),
            P("ep", None, "th"),
            P("ep", None, "th"),
            P("ep", None, "th"),
        ),
        check_vma=False,
    )
```

time: 508 us -> 403 us (0.79); the launches traced: 502 us -> 403 us
  Pallas kernels: 21.1 us -> 366 us
  waiting for transfers between devices: 185 us -> 0 us
  blocking collectives: 132 us -> 0 us
  matrix products: 90.2 us -> 9.65 us
  starting transfers between devices: 27.8 us -> 0 us
  between operations: 14.2 us -> 0.83 us
  local copies, waits for them, and re-layouts: 25.7 us -> 16.2 us
    pallas_call x1 -> x2, Pallas kernels: 21.1 us -> 366 us  [the longest x1 349 us: layer(): pl.pallas_call(layer_body, out_shape=[jax.ShapeDtypeStruct((3, width, col...]
    all_to_all x3 -> x0, blocking collectives: 125 us -> none  [the longest x1 70.5 us: local(): lax.all_to_all(rows_send, 'ep', split_axis=0, concat_axis=0, tiled=True)]
    all_to_all x4 -> x0, waiting for transfers between devices: 81.3 us -> none  [the longest x2 63 us: local(): lax.all_to_all(w, 'ep', split_axis=0, concat_axis=1, tiled=True)[0]]
    dot_general x11 -> x3, matrix products: 90.2 us -> 9.65 us  [the longest x1 5.04 us: local(): lax.dot_general(spread, back.reshape(PEERS * SROWS, -1), (((0,), (0,)), (...]
    reduce_scatter x1 -> x0, waiting for transfers between devices: 72.4 us -> none  [local(): lax.psum_scatter(partial_value.astype(jnp.bfloat16), 'th', scatter_dimens...]
    all_gather x2 -> x0, waiting for transfers between devices: 30.2 us -> none  [the longest x1 30.2 us: local(): lax.all_gather(rows_quarter[:, quarter:], 'th', axis=1, tiled=True)]
    all_to_all x4 -> x0, starting transfers between devices: 27.7 us -> none  [the longest x2 10.2 us: local(): lax.all_to_all(w, 'ep', split_axis=0, concat_axis=1, tiled=True)[0]]
    all_to_all x5 -> x0, local copies, waits for them, and re-layouts: 19.8 us -> none  [the longest x2 14.5 us: local(): lax.all_to_all(rows_send, 'ep', split_axis=0, concat_axis=0, tiled=True)]
  transfers between devices with their start and end apart: 7 -> 0, of which waited for: 6 -> 0; matrix products, arithmetic and copies ran while one was open for 10% -> 0% of each run, Pallas kernels for 4% -> 0%
where the time goes in v2:
time: 403 us
  Pallas kernels  366 us (91%)
  local copies, waits for them, and re-layouts  16.2 us (4%)
  other arithmetic  10.1 us (3%)
  matrix products  9.65 us (2%)
    pallas_call x1, Pallas kernels, layer(): pl.pallas_call(layer_body, out_shape=[jax.ShapeDtypeStruct((3, width, col...  349 us
    pallas_call x1, Pallas kernels, reorder(): pl.pallas_call(reorder_body, out_shape=jax.ShapeDtypeStruct((count, 3 * d...  16.6 us

profile of v2, /device:TPU:1, one launch (start us, length us, event | category | flops | bytes accessed | tf_op | source)
XLA Modules:
  0.0 402.7 jit_solution(16624850937951957859)
XLA Ops:
  0.7 0.8 select_reduce_fusion.2.order
  1.6 0.1 broadcast_add_fusion
  1.6 0.7 convert_element_type.41
  2.3 0.8 compare_reduce_fusion
  3.1 0.1 fusion.14
  3.2 0.8 fusion.15
  4.0 0.2 select_reduce_fusion.1
  4.3 0.1 copy.32
  4.4 0.7 broadcast_in_dim.47.gsend_ref
  5.1 0.1 iota_compare_fusion.2
  5.1 0.1 copy.25
  5.2 1.1 copy.26
  6.4 1.1 copy.27
  7.5 0.2 copy.28
  7.8 1.1 fusion.10.pack_ref
  8.8 1.4 fusion.9.packt_ref
  10.2 2.4 broadcast_and_fusion
  12.6 0.0 copy-start.4
  12.6 0.0 copy-start.1
  12.6 0.0 copy-start.2
  12.6 0.0 copy-start.3
  12.6 4.5 %fusion.4 = bf16[4608,512]{1,0:T(8,128)(2,1)} fusion(bf16[512,512]{1,0:T(8,128)(2,1)S(1)} %bitcast.34, pred[576,8,4,128]{3,2,1,0:T(4,128)(4,1)S(1)} %bitcast.31), kind=kOutput, calls=%fused_computation.4 | convolution fusion | flops 2418278400 | bytes 7602176 | tf_op jit(solution)/shard_map/dot_general | solution.py:498
  17.1 0.0 copy-done.4
  17.1 0.0 copy-done.1
  17.1 0.9 copy-done.2
  18.0 0.9 copy-done.3
  18.9 16.6 %shard_map.119.wsend_ref = bf16[32,384,384]{2,1,0:T(8,128)(2,1)S(1)} custom-call(s32[32]{0:T(128)S(1)} %select_reduce_fusion.2.order, bf16[32,128,384]{2,1,0:T(8,128)(2,1)S(1)} %copy-done.1, bf16[32,128,384]{2,1,0:T(8,128)(2,1)S(1)} %copy-done.2, bf16[32,128,384]{2,1,0:T(8,128)(2,1)S(1)} %copy-done.3), custom_call_target="tpu_custom_call" | custom-call | tf_op jit(solution)/shard_map/pallas_call | solution.py:68
  35.5 0.0 copy-start
  35.5 3.6 copy-done
  39.2 349.3 %shard_map.120 = (bf16[3,4096,384]{2,1,0:T(8,128)(2,1)}, bf16[32,144,256]{2,1,0:T(8,128)(2,1)}, bf16[32,16,128]{2,1,0:T(8,128)(2,1)}) custom-call(bf16[32,144,512]{2,1,0:T(8,128)(2,1)} %bitcast.30, bf16[32,16,128]{2,1,0:T(8,128)(2,1)} %broadcast_in_dim.47.gsend_ref, bf16[32,384,384]{2,1,0:T(8,128)(2,1)} %copy-done, bf16[4,144,576]{2,1,0:T(8,128)(2,1)} %fusion.10.pack_ref, ...), custom_call_target="tpu_custom_call" | custom-call | tf_op jit(solution)/shard_map/pallas_call | solution.py:438
  388.4 0.0 copy-start.5
  388.5 5.0 %fusion.11 = bf16[512,256]{1,0:T(8,128)(2,1)S(1)} fusion(bf16[4608,256]{1,0:T(8,128)(2,1)} %bitcast.40, pred[576,8,4,128]{3,2,1,0:T(4,128)(4,1)} %bitcast.32), kind=kOutput, calls=%fused_computation.12 | convolution fusion | flops 1208090624 | bytes 4980736 | tf_op jit(solution)/shard_map/dot_general | solution.py:513
  393.5 0.7 copy.33
  394.2 0.8 slice_convert_fusion
  395.1 0.1 copy.31
  395.2 0.2 select_reduce_fusion
  395.4 0.0 copy-done.5
  395.4 0.7 fusion.16
  396.1 6.6 %fusion.31 = (bf16[1,4096,384]{2,1,0:T(8,128)(2,1)}, bf16[1,4096,384]{2,1,0:T(8,128)(2,1)}, bf16[1,4096,384]{2,1,0:T(8,128)(2,1)}) fusion(bf16[3,4096,384]{2,1,0:T(8,128)(2,1)} %get-tuple-element.10), kind=kLoop, calls=%fused_computation.71 | loop fusion | bytes 18874368 | tf_op jit(solution)/shard_map/slice | solution.py:525
  (6 shorter events, 0.1 us)
Async XLA Ops:
  12.6 4.5 %copy-start.4 = (pred[32,4,36,4,128]{4,3,2,1,0:T(4,128)(4,1)}, pred[32,4,36,4,128]{4,3,2,1,0:T(4,128)(4,1)S(1)}, u32[]{:S(2)}) copy-start(pred[32,4,36,4,128]{4,3,2,1,0:T(4,128)(4,1)S(1)} %broadcast_and_fusion) | copy-start | bytes 7077892
  12.6 4.5 %copy-start.1 = (bf16[32,128,384]{2,1,0:T(8,128)(2,1)S(1)}, bf16[32,128,384]{2,1,0:T(8,128)(2,1)}, u32[]{:S(2)}) copy-start(bf16[32,128,384]{2,1,0:T(8,128)(2,1)} %gate_ref.1) | copy-start | bytes 9437188
  12.6 5.4 %copy-start.2 = (bf16[32,128,384]{2,1,0:T(8,128)(2,1)S(1)}, bf16[32,128,384]{2,1,0:T(8,128)(2,1)}, u32[]{:S(2)}) copy-start(bf16[32,128,384]{2,1,0:T(8,128)(2,1)} %up_ref.1) | copy-start | bytes 9437188
  12.6 6.3 %copy-start.3 = (bf16[32,128,384]{2,1,0:T(8,128)(2,1)S(1)}, bf16[32,128,384]{2,1,0:T(8,128)(2,1)}, u32[]{:S(2)}) copy-start(bf16[32,128,384]{2,1,0:T(8,128)(2,1)} %down_ref.1) | copy-start | bytes 9437188
  35.5 3.6 copy-start
  388.4 7.0 %copy-start.5 = (s32[128,8]{0,1:T(8,128)S(1)}, s32[128,8]{0,1:T(8,128)}, u32[]{:S(2)}) copy-start(s32[128,8]{0,1:T(8,128)} %param.11) | copy-start | bytes 12292

commit v3 on v2

--- a/solution.py
+++ b/solution.py
@@ -18,19 +18,20 @@
 BF16 = jnp.bfloat16
 
 
-def offset(k):
-    m = k // 2
-    return m % 4, (m // 4 + m % 4) % 4, k % 2
+def offset(core, k):
+    m, sign = k % 16, 1 + 2 * core
+    return m % 4 * sign % 4, (m // 4 + m % 4) % 4 * sign % 4, k // 16
 
 
 def peer_to(me, k):
-    dx, dy, dc = offset(k)
+    dx, dy, dc = offset(me % 2, k)
     return (me // 8 + dx) % 4 * 8 + ((me // 2) % 4 + dy) % 4 * 2 + (me % 2 + dc) % 2
 
 
 def peer_from(me, k):
-    dx, dy, dc = offset(k)
-    return (me // 8 + 4 - dx) % 4 * 8 + ((me // 2) % 4 + 4 - dy) % 4 * 2 + (me % 2 + dc) % 2
+    core = (me % 2 + k // 16) % 2
+    dx, dy, _ = offset(core, k)
+    return (me // 8 + 4 - dx) % 4 * 8 + ((me // 2) % 4 + 4 - dy) % 4 * 2 + core
 
 
 def reorder_body(order, gate_ref, up_ref, down_ref, out_ref, held, in_sems, out_sems):
@@ -47,7 +48,7 @@
     def write(k):
         return pltpu.make_async_copy(held.at[k], out_ref.at[k], out_sems.at[k])
 
-    @pl.loop(0, PEERS)
+    @pl.loop(0, PEERS, unroll=8)
     def _(k):
         for copy in reads(k):
             copy.start()
@@ -87,7 +88,7 @@
     rows_ref, gsend_ref, wsend_ref, pack_ref, packt_ref,
     gw_ref, back_ref, qback_ref,
     wv, xy, rr, gr, dab, acc, s1s, s1r, s2s, s2r, own, ret, qp, qr, qs, stage,
-    row_s, row_r, g_s, g_r, w_s, w_r, z_s, z_r, v_s, v_r, s1_s, s1_r, s2_s, s2_r,
+    row_s, row_r, g_s, g_r, w_s, w_r, z_s, z_r, v_s, v_r, s1_s, s1_r, s2_s, s2_r, d_s, d_r,
     b_s, b_r, q_s, q_r, qb_s, qb_r, o_s,
 ):
     me = lax.axis_index("ep")
@@ -138,16 +139,14 @@
     row_own.start()
     g_own.start()
 
-    @pl.loop(1, PEERS)
-    def _(k):
-        g_copy(k).start()
-        row_copy(k).start()
-
+    def send_rows(first, last):
+        @pl.loop(first, last)
+        def _(k):
+            g_copy(k).start()
+            row_copy(k).start()
+
+    send_rows(1, 3 * SET)
     w_own.start()
-
-    @pl.loop(1, PEERS)
-    def _(k):
-        w_copy(k).start()
 
     def z_copies(i):
         return (
@@ -177,31 +176,41 @@
     row_own.wait()
     g_own.wait()
 
-    @pl.loop(0, CHUNKS)
+    @pl.loop(0, SETS)
     def _(i):
-        for part in range(PER):
-            base = (i * PER + part) * SET
-            for n in range(SET):
-                k = base + n
-
-                @pl.when(k > 0)
-                def _():
-                    row_copy(k).wait_recv()
-                    g_copy(k).wait_recv()
-
-            arrived = rr[pl.ds(base, SET)].reshape(SET * SROWS, rr.shape[2])
-            wide = rr.shape[2]
-            for c in range(4):
-                piece = jnp.dot(pack_ref[c], arrived, preferred_element_type=F32).astype(BF16)
-                xy[th, i, c // 2, pl.ds(part * SROWS, SROWS), pl.ds(c % 2 * wide, wide)] = piece
+        for n in range(SET):
+            k = i * SET + n
+
+            @pl.when(k > 0)
+            def _():
+                row_copy(k).wait_recv()
+                g_copy(k).wait_recv()
+
+        @pl.when(i == 0)
+        def _():
+            send_rows(3 * SET, 6 * SET)
+
+        arrived = rr[pl.ds(i * SET, SET)].reshape(SET * SROWS, rr.shape[2])
+        wide = rr.shape[2]
+        for c in range(4):
+            piece = jnp.dot(pack_ref[c], arrived, preferred_element_type=F32).astype(BF16)
+            xy[th, i, c // 2, :, pl.ds(c % 2 * wide, wide)] = piece
         for copy in z_copies(i):
             copy.start()
+
+        @pl.when(i == 1)
+        def _():
+            send_rows(6 * SET, PEERS)
+
+            @pl.loop(1, PEERS)
+            def _(k):
+                w_copy(k).start()
 
         @pl.when(i > 0)
         def _():
             relay(i - 1)
 
-    relay(CHUNKS - 1)
+    relay(SETS - 1)
 
     w_own.wait()
 
@@ -245,8 +254,14 @@
 
     def s2_copies(i):
         return (
-            th_copy(s2s.at[i, 0], s2r.at[i, 0], s2_s.at[0, i], s2_r.at[0, i], right),
-            th_copy(s2s.at[i, 1], s2r.at[i, 1], s2_s.at[1, i], s2_r.at[1, i], left),
+            th_copy(s2s.at[i, 0, 0], s2r.at[i, 0, 0], s2_s.at[0, i], s2_r.at[0, i], right),
+            th_copy(s2s.at[i, 1, 1], s2r.at[i, 1, 1], s2_s.at[1, i], s2_r.at[1, i], left),
+        )
+
+    def d_copies(i):
+        return (
+            th_copy(s2s.at[i, 0, 1], s2r.at[i, 0, 1], d_s.at[0, i], d_r.at[0, i], right),
+            th_copy(s2s.at[i, 1, 0], s2r.at[i, 1, 0], d_s.at[1, i], d_r.at[1, i], left),
         )
 
     def b_copy(k):
@@ -257,13 +272,12 @@
     def combine(i):
         for n, copy in enumerate(s1_copies(i)):
             copy.wait_recv()
-            at = pl.ds(n * half, half)
-            s2s[i, n, :, at] = (s2s[i, n, :, at].astype(F32) + s1r[i, n].astype(F32)).astype(BF16)
+            s2s[i, n, n] = (s2s[i, n, n].astype(F32) + s1r[i, n].astype(F32)).astype(BF16)
         for copy in s2_copies(i):
             copy.start()
 
     def finish(i):
-        for copy in s2_copies(i):
+        for copy in (*d_copies(i), *s2_copies(i)):
             copy.wait_recv()
         strip = quarter // 4
         for part in range(PER):
@@ -271,11 +285,11 @@
             at = pl.ds(part * SROWS, SROWS)
             packed = jnp.zeros((SET * SROWS, strip), F32)
             for c in range(4):
-                span = pl.ds(c * strip, strip)
+                h, span = c // 2, pl.ds(c % 2 * strip, strip)
                 total = (
-                    own[i, at, span].astype(F32)
-                    + s2r[i, 0, at, span].astype(F32)
-                    + s2r[i, 1, at, span].astype(F32)
+                    own[i, h, at, span].astype(F32)
+                    + s2r[i, 0, h, at, span].astype(F32)
+                    + s2r[i, 1, h, at, span].astype(F32)
                 ).astype(BF16)
                 packed += jnp.dot(packt_ref[c], total, preferred_element_type=F32)
             ret[pl.ds(base, SET)] = packed.astype(BF16).reshape(SET, SROWS, strip)
@@ -294,12 +308,14 @@
 
     @pl.loop(0, CHUNKS)
     def _(i):
-        v_wait(i)
+        for part in range(PER):
+            v_wait(i * PER + part)
         acc[...] = jnp.zeros_like(acc)
 
         @pl.loop(0, 4)
         def _(j):
-            x, y = xy[j, i, 0], xy[j, i, 1]
+            x = xy[j, pl.ds(i * PER, PER), 0].reshape(CROWS, quarter)
+            y = xy[j, pl.ds(i * PER, PER), 1].reshape(CROWS, quarter)
             first = j * blocks
             acc[0] += jnp.dot(x, weight(0, first, blocks), preferred_element_type=F32)
             acc[1] += jnp.dot(x, weight(1, first, blocks), preferred_element_type=F32)
@@ -333,10 +349,15 @@
 
         @pl.loop(0, 2)
         def _(h):
-            span = pl.ds(pl.multiple_of(h * half, half), half)
-            s2s[i, 0, :, span] = partial(i, right, h)
-            s2s[i, 1, :, span] = partial(i, left, h)
-            own[i, :, span] = partial(i, th, h)
+            s2s[i, 0, 1 - h] = partial(i, right, 1 - h)
+            s2s[i, 1, h] = partial(i, left, h)
+
+            @pl.when(h == 0)
+            def _():
+                for copy in d_copies(i):
+                    copy.start()
+
+            own[i, h] = partial(i, th, h)
 
         @pl.when(i > 0)
         def _():
@@ -373,7 +394,7 @@
 
         span = pl.ds(pl.multiple_of(t % 2 * half, half), half)
         for n, kind in enumerate((0, 0, 1)):
-            rows = xy[t // 2, :, kind, :, span].reshape(CHUNKS * CROWS, half)
+            rows = xy[t // 2, :, kind, :, span].reshape(SETS * SROWS, half)
             hid = dab[n].reshape(CHUNKS * CROWS, cols)
             stage[t % 2, n] = lax.dot_general(
                 rows, hid, over_rows, preferred_element_type=F32
@@ -420,9 +441,14 @@
     for copy in q_copies:
         copy.wait_send()
 
+    @pl.loop(0, SETS)
+    def _(i):
+        for copy in (*z_copies(i), *v_copies(i)):
+            copy.wait_send()
+
     @pl.loop(0, CHUNKS)
     def _(i):
-        for copy in (*z_copies(i), *v_copies(i), *s1_copies(i), *s2_copies(i)):
+        for copy in (*s1_copies(i), *d_copies(i), *s2_copies(i)):
             copy.wait_send()
 
 
@@ -432,7 +458,7 @@
     strip = quarter // 4
     half = quarter // 2
     dma = pltpu.SemaphoreType.DMA
-    peer, ring = dma((PEERS,)), dma((2, CHUNKS))
+    peer, sets, ring = dma((PEERS,)), dma((2, SETS)), dma((2, CHUNKS))
     anywhere = pl.BlockSpec(memory_space=pl.ANY)
     inside = pl.BlockSpec(memory_space=pltpu.VMEM)
     return pl.pallas_call(
@@ -446,23 +472,23 @@
         out_specs=[anywhere] * 3,
         scratch_shapes=[
             pltpu.VMEM((PEERS, 3 * 128, cols), BF16),
-            pltpu.VMEM((4, CHUNKS, 2, CROWS, quarter), BF16),
+            pltpu.VMEM((4, SETS, 2, SROWS, quarter), BF16),
             pltpu.VMEM((PEERS, SROWS, wide), BF16),
             pltpu.VMEM((PEERS, 16, 128), BF16),
             pltpu.VMEM((3, CHUNKS, CROWS, cols), BF16),
             pltpu.VMEM((3, CROWS, cols), F32),
             pltpu.VMEM((CHUNKS, 2, CROWS, half), BF16),
             pltpu.VMEM((CHUNKS, 2, CROWS, half), BF16),
-            pltpu.VMEM((CHUNKS, 2, CROWS, quarter), BF16),
-            pltpu.VMEM((CHUNKS, 2, CROWS, quarter), BF16),
-            pltpu.VMEM((CHUNKS, CROWS, quarter), BF16),
+            pltpu.VMEM((CHUNKS, 2, 2, CROWS, half), BF16),
+            pltpu.VMEM((CHUNKS, 2, 2, CROWS, half), BF16),
+            pltpu.VMEM((CHUNKS, 2, CROWS, half), BF16),
             pltpu.VMEM((PEERS, SROWS, strip), BF16),
             pltpu.VMEM((SETS, 8, 128), F32),
             pltpu.VMEM((3, SETS, 8, 128), F32),
             pltpu.VMEM((PEERS, 16, 128), BF16),
             pltpu.VMEM((2, 3, half, cols), BF16),
             peer, peer, peer, peer, peer, peer,
-            ring, ring, ring, ring, ring, ring, ring, ring,
+            sets, sets, sets, sets, ring, ring, ring, ring, ring, ring,
             peer, peer, dma((3,)), dma((3,)), peer, peer, dma((2, 3)),
         ],
         compiler_params=pltpu.CompilerParams(

time: 403 us -> 341 us (0.85)
  Pallas kernels: 366 us -> 301 us
    pallas_call x1, Pallas kernels: 349 us -> 285 us  [layer(): pl.pallas_call(layer_body, out_shape=[jax.ShapeDtypeStruct((3, width, col...]
where the time goes in v3:
time: 341 us; the launch traced here: 338 us
  Pallas kernels  301 us (88%)
  local copies, waits for them, and re-layouts  16.2 us (5%)
  other arithmetic  10.1 us (3%)
  matrix products  9.64 us (3%)
    pallas_call x1, Pallas kernels, layer(): pl.pallas_call(layer_body, out_shape=[jax.ShapeDtypeStruct((3, width, col...  285 us
    pallas_call x1, Pallas kernels, reorder(): pl.pallas_call(reorder_body, out_shape=jax.ShapeDtypeStruct((count, 3 * d...  16.5 us
    unnamed x15, local copies, waits for them, and re-layouts  7.78 us

profile of v3, /device:TPU:1, one launch (start us, length us, event | category | flops | bytes accessed | tf_op | source)
XLA Modules:
  0.0 337.8 jit_solution(5882189217731930523)
XLA Ops:
  0.7 0.8 select_reduce_fusion.2.order
  1.6 0.1 broadcast_add_fusion
  1.7 0.7 convert_element_type.41
  2.3 0.8 compare_reduce_fusion
  3.1 0.1 fusion.14
  3.3 0.8 fusion.15
  4.0 0.2 select_reduce_fusion.1
  4.3 0.1 copy.32
  4.4 0.7 broadcast_in_dim.47.gsend_ref
  5.1 0.1 iota_compare_fusion.2
  5.2 0.1 copy.25
  5.2 1.1 copy.26
  6.4 1.1 copy.27
  7.5 0.2 copy.28
  7.8 1.1 fusion.10.pack_ref
  8.8 1.4 fusion.9.packt_ref
  10.2 2.4 broadcast_and_fusion
  12.6 0.0 copy-start.4
  12.6 0.0 copy-start.1
  12.6 0.0 copy-start.2
  12.6 0.0 copy-start.3
  12.6 4.5 %fusion.4 = bf16[4608,512]{1,0:T(8,128)(2,1)} fusion(bf16[512,512]{1,0:T(8,128)(2,1)S(1)} %bitcast.34, pred[576,8,4,128]{3,2,1,0:T(4,128)(4,1)S(1)} %bitcast.31), kind=kOutput, calls=%fused_computation.4 | convolution fusion | flops 2418278400 | bytes 7602176 | tf_op jit(solution)/shard_map/dot_general | solution.py:524
  17.1 0.0 copy-done.4
  17.1 0.0 copy-done.1
  17.1 0.9 copy-done.2
  18.0 0.9 copy-done.3
  18.9 16.5 %shard_map.119.wsend_ref = bf16[32,384,384]{2,1,0:T(8,128)(2,1)S(1)} custom-call(s32[32]{0:T(128)S(1)} %select_reduce_fusion.2.order, bf16[32,128,384]{2,1,0:T(8,128)(2,1)S(1)} %copy-done.1, bf16[32,128,384]{2,1,0:T(8,128)(2,1)S(1)} %copy-done.2, bf16[32,128,384]{2,1,0:T(8,128)(2,1)S(1)} %copy-done.3), custom_call_target="tpu_custom_call" | custom-call | tf_op jit(solution)/shard_map/pallas_call | solution.py:69
  35.4 0.0 copy-start
  35.4 3.6 %copy-done = bf16[32,384,384]{2,1,0:T(8,128)(2,1)} copy-done((bf16[32,384,384]{2,1,0:T(8,128)(2,1)}, bf16[32,384,384]{2,1,0:T(8,128)(2,1)S(1)}, u32[]{:S(2)}) %copy-start) | copy-done | bytes 9437208
  39.0 284.5 %shard_map.120 = (bf16[3,4096,384]{2,1,0:T(8,128)(2,1)}, bf16[32,144,256]{2,1,0:T(8,128)(2,1)}, bf16[32,16,128]{2,1,0:T(8,128)(2,1)}) custom-call(bf16[32,144,512]{2,1,0:T(8,128)(2,1)} %bitcast.30, bf16[32,16,128]{2,1,0:T(8,128)(2,1)} %broadcast_in_dim.47.gsend_ref, bf16[32,384,384]{2,1,0:T(8,128)(2,1)} %copy-done, bf16[4,144,576]{2,1,0:T(8,128)(2,1)} %fusion.10.pack_ref, ...), custom_call_target="tpu_custom_call" | custom-call | tf_op jit(solution)/shard_map/pallas_call | solution.py:464
  323.5 0.0 copy-start.5
  323.6 5.0 %fusion.11 = bf16[512,256]{1,0:T(8,128)(2,1)S(1)} fusion(bf16[4608,256]{1,0:T(8,128)(2,1)} %bitcast.40, pred[576,8,4,128]{3,2,1,0:T(4,128)(4,1)} %bitcast.32), kind=kOutput, calls=%fused_computation.12 | convolution fusion | flops 1208090624 | bytes 4980736 | tf_op jit(solution)/shard_map/dot_general | solution.py:539
  328.6 0.7 copy.33
  329.3 0.8 slice_convert_fusion
  330.2 0.1 copy.31
  330.3 0.2 select_reduce_fusion
  330.5 0.0 copy-done.5
  330.5 0.7 fusion.16
  331.2 6.6 %fusion.35 = (bf16[1,4096,384]{2,1,0:T(8,128)(2,1)}, bf16[1,4096,384]{2,1,0:T(8,128)(2,1)}, bf16[1,4096,384]{2,1,0:T(8,128)(2,1)}) fusion(bf16[3,4096,384]{2,1,0:T(8,128)(2,1)} %get-tuple-element.10), kind=kLoop, calls=%fused_computation.80 | loop fusion | bytes 18874368 | tf_op jit(solution)/shard_map/slice | solution.py:551
  (6 shorter events, 0.1 us)
Async XLA Ops:
  12.6 4.5 %copy-start.4 = (pred[32,4,36,4,128]{4,3,2,1,0:T(4,128)(4,1)}, pred[32,4,36,4,128]{4,3,2,1,0:T(4,128)(4,1)S(1)}, u32[]{:S(2)}) copy-start(pred[32,4,36,4,128]{4,3,2,1,0:T(4,128)(4,1)S(1)} %broadcast_and_fusion) | copy-start | bytes 7077892
  12.6 4.5 %copy-start.1 = (bf16[32,128,384]{2,1,0:T(8,128)(2,1)S(1)}, bf16[32,128,384]{2,1,0:T(8,128)(2,1)}, u32[]{:S(2)}) copy-start(bf16[32,128,384]{2,1,0:T(8,128)(2,1)} %gate_ref.1) | copy-start | bytes 9437188
  12.6 5.4 %copy-start.2 = (bf16[32,128,384]{2,1,0:T(8,128)(2,1)S(1)}, bf16[32,128,384]{2,1,0:T(8,128)(2,1)}, u32[]{:S(2)}) copy-start(bf16[32,128,384]{2,1,0:T(8,128)(2,1)} %up_ref.1) | copy-start | bytes 9437188
  12.6 6.3 %copy-start.3 = (bf16[32,128,384]{2,1,0:T(8,128)(2,1)S(1)}, bf16[32,128,384]{2,1,0:T(8,128)(2,1)}, u32[]{:S(2)}) copy-start(bf16[32,128,384]{2,1,0:T(8,128)(2,1)} %down_ref.1) | copy-start | bytes 9437188
  35.4 3.6 %copy-start = (bf16[32,384,384]{2,1,0:T(8,128)(2,1)}, bf16[32,384,384]{2,1,0:T(8,128)(2,1)S(1)}, u32[]{:S(2)}) copy-start(bf16[32,384,384]{2,1,0:T(8,128)(2,1)S(1)} %shard_map.119.wsend_ref) | copy-start | bytes 28311556
  323.5 7.0 %copy-start.5 = (s32[128,8]{0,1:T(8,128)S(1)}, s32[128,8]{0,1:T(8,128)}, u32[]{:S(2)}) copy-start(s32[128,8]{0,1:T(8,128)} %param.11) | copy-start | bytes 12292

commit v4 on v3

v4 whole, which is shorter than its diff:
```python
import jax
import jax.numpy as jnp
from jax import lax
from jax.experimental import pallas as pl
from jax.experimental.pallas import tpu as pltpu
from jax.sharding import PartitionSpec as P

CAP = 36
PEERS = 32
SET = 4
CHUNKS = 4
SETS = PEERS // SET
PER = SETS // CHUNKS
SROWS = SET * CAP
CROWS = PER * SROWS
MESH = pl.DeviceIdType.MESH
F32 = jnp.float32
BF16 = jnp.bfloat16


def offset(core, k):
    m, sign = k % 16, 1 + 2 * core
    return m % 4 * sign % 4, (m // 4 + m % 4) % 4 * sign % 4, k // 16


def peer_to(me, k):
    dx, dy, dc = offset(me % 2, k)
    return (me // 8 + dx) % 4 * 8 + ((me // 2) % 4 + dy) % 4 * 2 + (me % 2 + dc) % 2


def peer_from(me, k):
    core = (me % 2 + k // 16) % 2
    dx, dy, _ = offset(core, k)
    return (me // 8 + 4 - dx) % 4 * 8 + ((me // 2) % 4 + 4 - dy) % 4 * 2 + core


def layer_body(
    order_ref, tokens_ref, cot_ref, gates_ref, routing_ref, expert_ref, gate_ref, up_ref, down_ref,
    gw_ref, back_ref, tok_out, gates_out,
    wv, xy, rr, gr, gs, acc, s1s, s1r, s2s, s2r, own, qp, qr, qb, pool, bounce, pack,
    spots, shares, routed,
    row_s, row_r, g_s, g_r, w_s, w_r, z_s, z_r, v_s, v_r, s1_s, s1_r, s2_s, s2_r, d_s, d_r,
    b_s, b_r, q_s, q_r, qb_s, qb_r, o_s, p_s, l_s,
):
    me = lax.axis_index("ep")
    th = lax.axis_index("th")
    right, left, opp = (th + 1) % 4, (th + 3) % 4, (th + 2) % 4
    cols = wv.shape[2]
    over_last = (((1,), (1,)), ((), ()))
    over_rows = (((0,), (0,)), ((), ()))

    def ep_copy(src, dst, s, r, p):
        return pltpu.make_async_remote_copy(
            src_ref=src, dst_ref=dst, send_sem=s, recv_sem=r, device_id={"ep": p},
            device_id_type=MESH,
        )

    def th_copy(src, dst, s, r, p):
        return pltpu.make_async_remote_copy(
            src_ref=src, dst_ref=dst, send_sem=s, recv_sem=r, device_id={"th": p},
            device_id_type=MESH,
        )

    barrier = pltpu.get_barrier_semaphore()

    @pl.loop(1, PEERS)
    def _(k):
        pl.semaphore_signal(
            barrier, inc=1, device_id={"ep": peer_to(me, k)}, device_id_type=MESH
        )

    for p in (right, left, opp):
        pl.semaphore_signal(barrier, inc=1, device_id={"th": p}, device_id_type=MESH)
    def pool_copy(n):
        return pltpu.make_async_copy((gate_ref, up_ref, down_ref)[n], pool.at[:, pl.ds(0, 128)], p_s.at[n])

    pool_copy(0).start()

    tok_count = tokens_ref.shape[0]
    quarter = tokens_ref.shape[1]
    half = quarter // 2
    strip = quarter // 4
    pair = 2 * tok_count
    top_count = routing_ref.shape[0]
    expert = expert_ref[...]
    hits = jnp.zeros((PEERS, tok_count), F32)
    share = jnp.zeros((PEERS, tok_count), F32)
    for n in range(top_count):
        same = routing_ref[pl.ds(n, 1), :] == expert
        hits = jnp.where(same, 1.0, hits)
        share = jnp.where(same, gates_ref[pl.ds(n, 1), :], share)
    earlier = lax.broadcasted_iota(jnp.int32, (tok_count, tok_count), 0) < (
        lax.broadcasted_iota(jnp.int32, (tok_count, tok_count), 1)
    )
    rank = jnp.dot(hits.astype(BF16), earlier.astype(F32).astype(BF16), preferred_element_type=F32)
    for c in range(4):
        spot = jnp.where(hits > 0.5, rank + float(c * CAP), -1.0)
        spots[:, pl.ds(c * tok_count, tok_count)] = spot
    shares[...] = share
    for c in range(2):
        at = pl.ds(c * half, half)
        own[0, 0, pl.ds(c * tok_count, tok_count), :] = tokens_ref[:, at]
        own[0, 1, pl.ds(c * tok_count, tok_count), :] = cot_ref[:, at]
    wide_row = lax.broadcasted_iota(jnp.int32, (SROWS, SET * SROWS), 0)
    wide_spot = lax.broadcasted_iota(jnp.int32, (SROWS, SET * SROWS), 1)
    for m in range(1, SET):
        wide_spot = wide_spot - jnp.where(wide_row >= m * CAP, SROWS - CAP, 0)
    for c in range(4):
        pack[c] = (wide_spot == wide_row + c * CAP).astype(F32).astype(BF16)
    row_ids = lax.broadcasted_iota(jnp.int32, (SROWS, 4 * tok_count), 0).astype(F32)

    def one_hot(k):
        return (row_ids == spots[pl.ds(k, 1), :]).astype(F32).astype(BF16)

    pl.semaphore_wait(barrier, PEERS - 1 + 3)

    def row_slot(k):
        return s2s.at[k // 8, k // 4 % 2, k // 2 % 2, pl.ds(k % 2 * SROWS, SROWS)]

    def row_copy(k):
        return ep_copy(row_slot(k), rr.at[k], row_s.at[k], row_r.at[k], peer_to(me, k))

    def g_copy(k):
        return ep_copy(gs.at[k], gr.at[k], g_s.at[k], g_r.at[k], peer_to(me, k))

    def build(k):
        chosen = one_hot(k)
        block = jnp.dot(chosen[:, :pair], own[0, 0, :pair, :], preferred_element_type=F32)
        block = block + jnp.dot(chosen[:, pair:], own[0, 1, :pair, :], preferred_element_type=F32)
        s2s[k // 8, k // 4 % 2, k // 2 % 2, pl.ds(pl.multiple_of(k % 2 * SROWS, 16), SROWS)] = (
            block.astype(BF16)
        )
        mine = jnp.broadcast_to(shares[pl.ds(k, 1), :], (16, tok_count)).astype(BF16)
        gs[k] = lax.dot_general(
            mine, chosen[:128, :tok_count], over_last, preferred_element_type=F32
        ).astype(BF16)

    def w_copy(n, k):
        return ep_copy(
            bounce.at[n % 2, k], wv.at[me, pl.ds(n * 128, 128)], w_s.at[n, k], w_r.at[n, k],
            peer_to(me, k),
        )

    def w_wait(n, k):
        s = peer_from(me, k)
        ep_copy(
            bounce.at[n % 2, k], wv.at[s, pl.ds(n * 128, 128)], w_s.at[n, k], w_r.at[n, k], s
        ).wait_recv()

    def w_own(n):
        return pltpu.make_async_copy(
            bounce.at[n % 2, 0], wv.at[me, pl.ds(n * 128, 128)], w_r.at[n, 0]
        )

    def send_weights(n):
        pool_copy(n).wait()

        @pl.loop(0, PEERS)
        def _(k):
            bounce[n % 2, k] = pool[order_ref[k]][:128]

            @pl.when(k > 0)
            def _():
                w_copy(n, k).start()

        w_own(n).start()
        if n < 2:
            pool_copy(n + 1).start()

    def wait_weights(n):
        w_own(n).wait()

        @pl.loop(1, PEERS)
        def _(k):
            w_copy(n, k).wait_send()

    row_own = pltpu.make_async_copy(row_slot(0), rr.at[0], row_r.at[0])
    g_own = pltpu.make_async_copy(gs.at[0], gr.at[0], g_r.at[0])

    def send_rows(first, last):
        @pl.loop(first, last)
        def _(k):
            build(k)
            g_copy(k).start()
            row_copy(k).start()

    build(0)
    row_own.start()
    g_own.start()
    send_rows(1, 3 * SET)

    def z_copies(i):
        return (
            th_copy(xy.at[th, i], xy.at[th, i], z_s.at[0, i], z_r.at[0, i], right),
            th_copy(xy.at[th, i], xy.at[th, i], z_s.at[1, i], z_r.at[1, i], left),
        )

    def z_wait(i):
        th_copy(xy.at[left, i], xy.at[left, i], z_s.at[0, i], z_r.at[0, i], left).wait_recv()
        th_copy(xy.at[right, i], xy.at[right, i], z_s.at[1, i], z_r.at[1, i], right).wait_recv()

    def v_copies(i):
        return (
            th_copy(xy.at[left, i, 0], xy.at[left, i, 0], v_s.at[0, i], v_r.at[0, i], right),
            th_copy(xy.at[right, i, 1], xy.at[right, i, 1], v_s.at[1, i], v_r.at[1, i], left),
        )

    def v_wait(i):
        th_copy(xy.at[opp, i, 0], xy.at[opp, i, 0], v_s.at[0, i], v_r.at[0, i], left).wait_recv()
        th_copy(xy.at[opp, i, 1], xy.at[opp, i, 1], v_s.at[1, i], v_r.at[1, i], right).wait_recv()

    def relay(i):
        z_wait(i)
        for copy in v_copies(i):
            copy.start()

    row_own.wait()
    g_own.wait()

    @pl.loop(0, SETS)
    def _(i):
        for n in range(SET):
            k = i * SET + n

            @pl.when(k > 0)
            def _():
                row_copy(k).wait_recv()
                g_copy(k).wait_recv()

        @pl.when(i == 0)
        def _():
            send_rows(3 * SET, 6 * SET)

        arrived = rr[pl.ds(i * SET, SET)].reshape(SET * SROWS, rr.shape[2])
        wide = rr.shape[2]
        for c in range(4):
            piece = jnp.dot(pack[c], arrived, preferred_element_type=F32).astype(BF16)
            xy[th, i, c // 2, :, pl.ds(c % 2 * wide, wide)] = piece
        for copy in z_copies(i):
            copy.start()

        @pl.when(i == 1)
        def _():
            send_rows(6 * SET, PEERS)
            send_weights(0)

        @pl.when(i == 2)
        def _():
            send_weights(1)

        @pl.when(i == 5)
        def _():
            wait_weights(0)
            send_weights(2)

        @pl.when(i > 0)
        def _():
            relay(i - 1)

    relay(SETS - 1)

    for n in (1, 2):
        wait_weights(n)

    @pl.loop(1, PEERS)
    def _(k):
        for n in range(3):
            w_wait(n, k)
        row_copy(k).wait_send()
        g_copy(k).wait_send()

    blocks = quarter // 128

    def weight(n, first, count):
        return wv[pl.ds(first, count), pl.ds(n * 128, 128), :].reshape(count * 128, cols)

    def hidden_rows(n, first, count):
        return pool[pl.ds(n * SETS + first, count)].reshape(count * SROWS, cols)

    def partial(i, j, h):
        da, db = hidden_rows(0, i * PER, PER), hidden_rows(1, i * PER, PER)
        first = j * blocks + h * (blocks // 2)
        value = lax.dot_general(
            da, weight(0, first, blocks // 2), over_last, preferred_element_type=F32
        ) + lax.dot_general(
            db, weight(1, first, blocks // 2), over_last, preferred_element_type=F32
        )
        return value.astype(BF16)

    row_at = lax.broadcasted_iota(jnp.int32, (SROWS, 128), 0)
    lane_at = lax.broadcasted_iota(jnp.int32, (SROWS, 128), 1)
    source_at = (
        (row_at >= CAP).astype(jnp.int32)
        + (row_at >= 2 * CAP).astype(jnp.int32)
        + (row_at >= 3 * CAP).astype(jnp.int32)
    )
    in_place = lane_at == row_at - source_at * CAP

    def s1_copies(i):
        return (
            th_copy(s1s.at[i % 2, 0], s1r.at[i, 0], s1_s.at[0, i], s1_r.at[0, i], right),
            th_copy(s1s.at[i % 2, 1], s1r.at[i, 1], s1_s.at[1, i], s1_r.at[1, i], left),
        )

    def s2_copies(i):
        return (
            th_copy(s2s.at[i, 0, 0], s2r.at[i, 0, 0], s2_s.at[0, i], s2_r.at[0, i], right),
            th_copy(s2s.at[i, 1, 1], s2r.at[i, 1, 1], s2_s.at[1, i], s2_r.at[1, i], left),
        )

    def d_copies(i):
        return (
            th_copy(s2s.at[i, 0, 1], s2r.at[i, 0, 1], d_s.at[0, i], d_r.at[0, i], right),
            th_copy(s2s.at[i, 1, 0], s2r.at[i, 1, 0], d_s.at[1, i], d_r.at[1, i], left),
        )

    def b_copy(k):
        return ep_copy(
            rr.at[k, :, pl.ds(0, strip)], back_ref.at[k], b_s.at[k], b_r.at[k], peer_from(me, k)
        )

    b_own = pltpu.make_async_copy(rr.at[0, :, pl.ds(0, strip)], back_ref.at[0], b_r.at[0])

    def combine(i):
        for n, copy in enumerate(s1_copies(i)):
            copy.wait_recv()
            s2s[i, n, n] = (s2s[i, n, n].astype(F32) + s1r[i, n].astype(F32)).astype(BF16)
        for copy in s2_copies(i):
            copy.start()

    def finish(i):
        for copy in (*d_copies(i), *s2_copies(i)):
            copy.wait_recv()
        for part in range(PER):
            base = (i * PER + part) * SET
            at = pl.ds(part * SROWS, SROWS)
            packed = jnp.zeros((SET * SROWS, strip), F32)
            for c in range(4):
                h, span = c // 2, pl.ds(c % 2 * strip, strip)
                total = (
                    own[i % 3, h, at, span].astype(F32)
                    + s2r[i, 0, h, at, span].astype(F32)
                    + s2r[i, 1, h, at, span].astype(F32)
                ).astype(BF16)
                packed += lax.dot_general(
                    pack[c], total, over_rows, preferred_element_type=F32
                )
            rr[pl.ds(base, SET), :, pl.ds(0, strip)] = packed.astype(BF16).reshape(
                SET, SROWS, strip
            )
            for n in range(SET):
                k = base + n

                @pl.when(k > 0)
                def _():
                    b_copy(k).start()

                @pl.when(k == 0)
                def _():
                    b_own.start()

    qp[...] = jnp.zeros_like(qp)

    @pl.loop(0, CHUNKS)
    def _(i):
        for part in range(PER):
            v_wait(i * PER + part)
        acc[...] = jnp.zeros_like(acc)

        @pl.loop(0, 4)
        def _(j):
            x = xy[j, pl.ds(i * PER, PER), 0].reshape(CROWS, quarter)
            y = xy[j, pl.ds(i * PER, PER), 1].reshape(CROWS, quarter)
            first = j * blocks
            acc[0] += jnp.dot(x, weight(0, first, blocks), preferred_element_type=F32)
            acc[1] += jnp.dot(x, weight(1, first, blocks), preferred_element_type=F32)
            acc[2] += jnp.dot(y, weight(2, first, blocks), preferred_element_type=F32)

        for part in range(PER):
            s = i * PER + part
            at = pl.ds(part * SROWS, SROWS)
            gate = jnp.zeros((SROWS, 128), F32)
            for n in range(SET):
                one = gr[s * SET + n].astype(F32)[0:1, :]
                gate = jnp.where(in_place & (source_at == n), one, gate)
            g = jnp.sum(gate, axis=1, keepdims=True)
            a, b, u = acc[0, at], acc[1, at], acc[2, at]
            sig = jax.nn.sigmoid(a)
            silu = a * sig
            hidden = silu * b
            dh = g * u
            pool[0 * SETS + s] = (dh * b * sig * (1.0 + a * (1.0 - sig))).astype(BF16)
            pool[1 * SETS + s] = (dh * silu).astype(BF16)
            pool[2 * SETS + s] = (g * hidden).astype(BF16)
            q = jnp.sum(u * hidden, axis=1, keepdims=True)
            for n in range(SET):
                mine = jnp.where(in_place & (source_at == n), q, 0.0)
                qp[s, pl.ds(n, 1), :] = jnp.sum(mine, axis=0, keepdims=True)

        @pl.when(i > 1)
        def _():
            for copy in s1_copies(i - 2):
                copy.wait_send()

        s1s[i % 2, 0] = partial(i, opp, 0)
        s1s[i % 2, 1] = partial(i, opp, 1)
        for copy in s1_copies(i):
            copy.start()

        @pl.loop(0, 2)
        def _(h):
            s2s[i, 0, 1 - h] = partial(i, right, 1 - h)
            s2s[i, 1, h] = partial(i, left, h)

            @pl.when(h == 0)
            def _():
                for copy in d_copies(i):
                    copy.start()

            own[i % 3, h] = partial(i, th, h)

        @pl.when(i > 0)
        def _():
            combine(i - 1)

        @pl.when(i > 1)
        def _():
            finish(i - 2)

    combine(CHUNKS - 1)

    q_copies = tuple(
        th_copy(qp, qr.at[n], q_s.at[n], q_r.at[n], p) for n, p in enumerate((right, left, opp))
    )
    for copy in q_copies:
        copy.start()
    finish(CHUNKS - 2)

    tile = half // 128

    def out_copies(t):
        return tuple(
            pltpu.make_async_copy(
                bounce.at[t % 2, pl.ds(n * tile, tile)], gw_ref.at[n, pl.ds(t * tile, tile)],
                o_s.at[t % 2, n],
            )
            for n in range(3)
        )

    def weight_grads(t):
        @pl.when(t > 1)
        def _():
            for copy in out_copies(t - 2):
                copy.wait()

        span = pl.ds(pl.multiple_of(t % 2 * half, half), half)
        for n, kind in enumerate((0, 0, 1)):
            rows = xy[t // 2, :, kind, :, span].reshape(SETS * SROWS, half)
            hid = hidden_rows(n, 0, SETS)
            value = lax.dot_general(rows, hid, over_rows, preferred_element_type=F32)
            bounce[t % 2, pl.ds(n * tile, tile)] = value.astype(BF16).reshape(tile, 128, cols)
        for copy in out_copies(t):
            copy.start()

    pl.loop(0, 4)(weight_grads)

    finish(CHUNKS - 1)
    for copy in q_copies:
        copy.wait_recv()

    def qb_copy(k):
        return ep_copy(gs.at[k], qb.at[k], qb_s.at[k], qb_r.at[k], peer_from(me, k))

    qb_own = pltpu.make_async_copy(gs.at[0], qb.at[0], qb_r.at[0])
    for s in range(SETS):
        total = qp[s] + qr[0, s] + qr[1, s] + qr[2, s]
        for n in range(SET):
            gs[s * SET + n] = jnp.broadcast_to(total[n : n + 1, :], (16, 128)).astype(BF16)
    qb_own.start()

    @pl.loop(1, PEERS)
    def _(k):
        qb_copy(k).start()

    pl.loop(4, 8)(weight_grads)
    for t in (6, 7):
        for copy in out_copies(t):
            copy.wait()

    def load(k):
        return pltpu.make_async_copy(back_ref.at[k], rr.at[k, :, pl.ds(strip, strip)], l_s.at[k])

    b_own.wait()
    load(0).start()

    @pl.loop(1, PEERS)
    def _(k):
        b_copy(k).wait_recv()
        load(k).start()

    qb_own.wait()

    for m in range(2):
        acc[m, pl.ds(0, pair), pl.ds(0, strip)] = jnp.zeros((pair, strip), F32)

    @pl.loop(0, PEERS)
    def _(k):
        @pl.when(k > 0)
        def _():
            qb_copy(k).wait_recv()

        load(k).wait()
        chosen = one_hot(k)
        found = jnp.dot(qb[k], chosen[:128, :tok_count], preferred_element_type=F32)
        routed[pl.ds(k, 1), :] = found[0:1, :]
        for m in range(2):
            acc[m, pl.ds(0, pair), pl.ds(0, strip)] += lax.dot_general(
                chosen[:, m * pair : (m + 1) * pair], rr[k, :, pl.ds(strip, strip)], over_rows,
                preferred_element_type=F32,
            )

    for c in range(4):
        tok_out[:, pl.ds(c * strip, strip)] = acc[
            c // 2, pl.ds(c % 2 * tok_count, tok_count), pl.ds(0, strip)
        ].astype(BF16)
    terms = routed[...]
    for n in range(top_count):
        same = routing_ref[pl.ds(n, 1), :] == expert
        gates_out[pl.ds(n, 1), :] = jnp.sum(jnp.where(same, terms, 0.0), axis=0, keepdims=True)

    @pl.loop(1, PEERS)
    def _(k):
        b_copy(k).wait_send()
        qb_copy(k).wait_send()

    for copy in q_copies:
        copy.wait_send()

    @pl.loop(0, SETS)
    def _(i):
        for copy in (*z_copies(i), *v_copies(i)):
            copy.wait_send()

    @pl.loop(0, CHUNKS)
    def _(i):
        for copy in (*d_copies(i), *s2_copies(i)):
            copy.wait_send()

    for i in (CHUNKS - 2, CHUNKS - 1):
        for copy in s1_copies(i):
            copy.wait_send()


def local(tokens, cotangent, gates, routing, new_slot, gate_old, up_old, down_old):
    tok_count, top_count = routing.shape
    quarter = tokens.shape[1]
    depth, cols = gate_old.shape[1:]
    ids = jnp.arange(PEERS, dtype=jnp.int32)
    expert = peer_to(lax.axis_index("ep"), ids)
    order = jnp.sum(
        (new_slot[None, :] == expert[:, None]).astype(jnp.int32) * ids[None, :], axis=1
    )
    half = quarter // 2
    strip = quarter // 4
    dma = pltpu.SemaphoreType.DMA
    peer, three = dma((PEERS,)), dma((3, PEERS))
    sets, ring = dma((2, SETS)), dma((2, CHUNKS))
    anywhere = pl.BlockSpec(memory_space=pl.ANY)
    inside = pl.BlockSpec(memory_space=pltpu.VMEM)
    grads, _, grad_tokens, grad_gates = pl.pallas_call(
        layer_body,
        out_shape=[
            jax.ShapeDtypeStruct((3, PEERS, depth, cols), BF16),
            jax.ShapeDtypeStruct((PEERS, SROWS, strip), BF16),
            jax.ShapeDtypeStruct(tokens.shape, BF16),
            jax.ShapeDtypeStruct((top_count, tok_count), F32),
        ],
        in_specs=[pl.BlockSpec(memory_space=pltpu.SMEM)] + [inside] * 5 + [anywhere] * 3,
        out_specs=[anywhere] * 2 + [inside] * 2,
        scratch_shapes=[
            pltpu.VMEM((PEERS, 3 * depth, cols), BF16),
            pltpu.VMEM((4, SETS, 2, SROWS, quarter), BF16),
            pltpu.VMEM((PEERS, SROWS, half), BF16),
            pltpu.VMEM((PEERS, 16, 128), BF16),
            pltpu.VMEM((PEERS, 16, 128), BF16),
            pltpu.VMEM((3, CROWS, cols), F32),
            pltpu.VMEM((2, 2, CROWS, half), BF16),
            pltpu.VMEM((CHUNKS, 2, CROWS, half), BF16),
            pltpu.VMEM((CHUNKS, 2, 2, CROWS, half), BF16),
            pltpu.VMEM((CHUNKS, 2, 2, CROWS, half), BF16),
            pltpu.VMEM((3, 2, CROWS, half), BF16),
            pltpu.VMEM((SETS, 8, 128), F32),
            pltpu.VMEM((3, SETS, 8, 128), F32),
            pltpu.VMEM((PEERS, 16, 128), BF16),
            pltpu.VMEM((PEERS, SROWS, cols), BF16),
            pltpu.VMEM((2, PEERS, depth, cols), BF16),
            pltpu.VMEM((4, SROWS, SET * SROWS), BF16),
            pltpu.VMEM((PEERS, 4 * tok_count), F32),
            pltpu.VMEM((PEERS, tok_count), F32),
            pltpu.VMEM((PEERS, tok_count), F32),
            peer, peer, peer, peer, three, three,
            sets, sets, sets, sets, ring, ring, ring, ring, ring, ring,
            peer, peer, dma((3,)), dma((3,)), peer, peer, dma((2, 3)), dma((3,)), peer,
        ],
        compiler_params=pltpu.CompilerParams(
            collective_id=0, has_side_effects=True, vmem_limit_bytes=63 * 2**20
        ),
    )(
        order, tokens, cotangent, gates.astype(F32).T, routing.T,
        jnp.broadcast_to(expert[:, None], (PEERS, tok_count)), gate_old, up_old, down_old,
    )
    grads = grads.reshape(3, PEERS * depth, cols)
    return (grad_tokens, grad_gates.T.astype(BF16), grads[0:1], grads[1:2], grads[2:3])


def solution(mesh):
    placed = (
        P("ep", "th"),
        P("ep", "th"),
        P("ep", None),
        P("ep", None),
        P(),
        P(None, "ep", "th"),
        P(None, "ep", "th"),
        P(None, "ep", "th"),
    )
    return jax.shard_map(
        local,
        mesh=mesh,
        in_specs=placed,
        out_specs=(
            P("ep", "th"),
            P("ep", None),
            P("ep", None, "th"),
            P("ep", None, "th"),
            P("ep", None, "th"),
        ),
        check_vma=False,
    )
```

time: 341 us -> 313 us (0.918)
  matrix products: 9.64 us -> 0 us
  local copies, waits for them, and re-layouts: 16.2 us -> 7.97 us
  other arithmetic: 10.1 us -> 3.92 us
  Pallas kernels: 301 us -> 295 us
    dot_general x3 -> x0, matrix products: 9.64 us -> none  [the longest x1 5.04 us: local(): lax.dot_general(spread, back.reshape(PEERS * SROWS, -1), (((0,), (0,)), (...]
    unnamed x15 -> x3, local copies, waits for them, and re-layouts: 7.78 us -> 0.71 us
    pallas_call x2 -> x1, Pallas kernels: 301 us -> 295 us  [local(): pl.pallas_call(layer_body, out_shape=[jax.ShapeDtypeStruct((3, PEERS, dep...]
where the time goes in v4:
time: 313 us; the launch traced here: 307 us
  Pallas kernels  295 us (94%)
  local copies, waits for them, and re-layouts  7.97 us (3%)
  other arithmetic  3.92 us (1%)
    pallas_call x1, Pallas kernels, local(): pl.pallas_call(layer_body, out_shape=[jax.ShapeDtypeStruct((3, PEERS, dep...  295 us
    slice x1, local copies, waits for them, and re-layouts, local(): grads[2:3]  6.59 us

profile of v4, /device:TPU:1, one launch (start us, length us, event | category | flops | bytes accessed | tf_op | source)
XLA Modules:
  0.0 307.3 jit_solution(13203823592738485141)
XLA Ops:
  0.7 1.4 select_reduce_fusion.order_ref
  2.1 1.3 convert_bitcast_fusion.gates_ref
  3.3 0.7 broadcast_in_dim.2.expert_ref
  4.0 294.7 %shard_map.119 = (bf16[3,32,128,384]{3,2,1,0:T(8,128)(2,1)}, bf16[32,144,256]{2,1,0:T(8,128)(2,1)}, bf16[128,1024]{1,0:T(8,128)(2,1)}, f32[8,128]{1,0:T(8,128)}) custom-call(s32[32]{0:T(128)} %select_reduce_fusion.order_ref, bf16[128,1024]{1,0:T(8,128)(2,1)} %tokens_ref.1, bf16[128,1024]{1,0:T(8,128)(2,1)} %cot_ref.1, ...), custom_call_target="tpu_custom_call" | custom-call | tf_op jit(solution)/shard_map/pallas_call | solution.py:570
  298.7 1.3 convert_bitcast_fusion.1
  300.0 0.0 copy-start
  300.0 6.6 %fusion.14 = (bf16[1,32,128,384]{3,2,1,0:T(8,128)(2,1)}, bf16[1,32,128,384]{3,2,1,0:T(8,128)(2,1)}, bf16[1,32,128,384]{3,2,1,0:T(8,128)(2,1)}) fusion(bf16[3,32,128,384]{3,2,1,0:T(8,128)(2,1)} %get-tuple-element.10), kind=kLoop, calls=%fused_computation.44 | loop fusion | bytes 18874368 | tf_op jit(solution)/shard_map/slice | solution.py:613
  306.6 0.0 copy-done
  306.6 0.7 copy.14
  (1 shorter events, 0.0 us)
Async XLA Ops:
  300.0 6.6 %copy-start = (bf16[128,1024]{1,0:T(8,128)(2,1)S(1)}, bf16[128,1024]{1,0:T(8,128)(2,1)}, u32[]{:S(2)}) copy-start(bf16[128,1024]{1,0:T(8,128)(2,1)} %get-tuple-element.19) | copy-start | bytes 786436

commit v5 on v4

--- a/solution.py
+++ b/solution.py
@@ -8,7 +8,7 @@
 CAP = 36
 PEERS = 32
 SET = 4
-CHUNKS = 4
+CHUNKS = 8
 SETS = PEERS // SET
 PER = SETS // CHUNKS
 SROWS = SET * CAP
@@ -38,7 +38,7 @@
     order_ref, tokens_ref, cot_ref, gates_ref, routing_ref, expert_ref, gate_ref, up_ref, down_ref,
     gw_ref, back_ref, tok_out, gates_out,
     wv, xy, rr, gr, gs, acc, s1s, s1r, s2s, s2r, own, qp, qr, qb, pool, bounce, pack,
-    spots, shares, routed,
+    sums, spots, shares, routed,
     row_s, row_r, g_s, g_r, w_s, w_r, z_s, z_r, v_s, v_r, s1_s, s1_r, s2_s, s2_r, d_s, d_r,
     b_s, b_r, q_s, q_r, qb_s, qb_r, o_s, p_s, l_s,
 ):
@@ -99,8 +99,8 @@
     shares[...] = share
     for c in range(2):
         at = pl.ds(c * half, half)
-        own[0, 0, pl.ds(c * tok_count, tok_count), :] = tokens_ref[:, at]
-        own[0, 1, pl.ds(c * tok_count, tok_count), :] = cot_ref[:, at]
+        own[0, c, pl.ds(0, tok_count), :] = tokens_ref[:, at]
+        own[1, c, pl.ds(0, tok_count), :] = cot_ref[:, at]
     wide_row = lax.broadcasted_iota(jnp.int32, (SROWS, SET * SROWS), 0)
     wide_spot = lax.broadcasted_iota(jnp.int32, (SROWS, SET * SROWS), 1)
     for m in range(1, SET):
@@ -115,7 +115,7 @@
     pl.semaphore_wait(barrier, PEERS - 1 + 3)
 
     def row_slot(k):
-        return s2s.at[k // 8, k // 4 % 2, k // 2 % 2, pl.ds(k % 2 * SROWS, SROWS)]
+        return s2s.at[k // 4, k // 2 % 2, k % 2]
 
     def row_copy(k):
         return ep_copy(row_slot(k), rr.at[k], row_s.at[k], row_r.at[k], peer_to(me, k))
@@ -125,11 +125,9 @@
 
     def build(k):
         chosen = one_hot(k)
-        block = jnp.dot(chosen[:, :pair], own[0, 0, :pair, :], preferred_element_type=F32)
-        block = block + jnp.dot(chosen[:, pair:], own[0, 1, :pair, :], preferred_element_type=F32)
-        s2s[k // 8, k // 4 % 2, k // 2 % 2, pl.ds(pl.multiple_of(k % 2 * SROWS, 16), SROWS)] = (
-            block.astype(BF16)
-        )
+        held = own[pl.ds(0, 2), :, pl.ds(0, tok_count), :].reshape(4 * tok_count, half)
+        block = jnp.dot(chosen, held, preferred_element_type=F32).astype(BF16)
+        s2s[k // 4, k // 2 % 2, k % 2] = block
         mine = jnp.broadcast_to(shares[pl.ds(k, 1), :], (16, tok_count)).astype(BF16)
         gs[k] = lax.dot_general(
             mine, chosen[:128, :tok_count], over_last, preferred_element_type=F32
@@ -427,14 +425,11 @@
         def _():
             finish(i - 2)
 
-    combine(CHUNKS - 1)
-
     q_copies = tuple(
         th_copy(qp, qr.at[n], q_s.at[n], q_r.at[n], p) for n, p in enumerate((right, left, opp))
     )
     for copy in q_copies:
         copy.start()
-    finish(CHUNKS - 2)
 
     tile = half // 128
 
@@ -463,8 +458,10 @@
             copy.start()
 
     pl.loop(0, 4)(weight_grads)
-
-    finish(CHUNKS - 1)
+    combine(CHUNKS - 1)
+    finish(CHUNKS - 2)
+    pl.loop(4, 6)(weight_grads)
+
     for copy in q_copies:
         copy.wait_recv()
 
@@ -482,46 +479,54 @@
     def _(k):
         qb_copy(k).start()
 
-    pl.loop(4, 8)(weight_grads)
+    def load(k):
+        return pltpu.make_async_copy(back_ref.at[k], rr.at[k, :, pl.ds(strip, strip)], l_s.at[k])
+
+    qb_own.wait()
+
+    for m in range(2):
+        sums[m] = jnp.zeros((pair, strip), F32)
+
+    def sum_tokens(first, last):
+        @pl.loop(first, last)
+        def _(k):
+            @pl.when(k > 0)
+            def _():
+                b_copy(k).wait_recv()
+
+            @pl.when(k == 0)
+            def _():
+                b_own.wait()
+
+            load(k).start()
+
+        @pl.loop(first, last)
+        def _(k):
+            @pl.when(k > 0)
+            def _():
+                qb_copy(k).wait_recv()
+
+            load(k).wait()
+            chosen = one_hot(k)
+            found = jnp.dot(qb[k], chosen[:128, :tok_count], preferred_element_type=F32)
+            routed[pl.ds(k, 1), :] = found[0:1, :]
+            for m in range(2):
+                sums[m] += lax.dot_general(
+                    chosen[:, m * pair : (m + 1) * pair], rr[k, :, pl.ds(strip, strip)], over_rows,
+                    preferred_element_type=F32,
+                )
+
+    sum_tokens(0, PEERS // 2)
+    finish(CHUNKS - 1)
+    pl.loop(6, 8)(weight_grads)
     for t in (6, 7):
         for copy in out_copies(t):
             copy.wait()
 
-    def load(k):
-        return pltpu.make_async_copy(back_ref.at[k], rr.at[k, :, pl.ds(strip, strip)], l_s.at[k])
-
-    b_own.wait()
-    load(0).start()
-
-    @pl.loop(1, PEERS)
-    def _(k):
-        b_copy(k).wait_recv()
-        load(k).start()
-
-    qb_own.wait()
-
-    for m in range(2):
-        acc[m, pl.ds(0, pair), pl.ds(0, strip)] = jnp.zeros((pair, strip), F32)
-
-    @pl.loop(0, PEERS)
-    def _(k):
-        @pl.when(k > 0)
-        def _():
-            qb_copy(k).wait_recv()
-
-        load(k).wait()
-        chosen = one_hot(k)
-        found = jnp.dot(qb[k], chosen[:128, :tok_count], preferred_element_type=F32)
-        routed[pl.ds(k, 1), :] = found[0:1, :]
-        for m in range(2):
-            acc[m, pl.ds(0, pair), pl.ds(0, strip)] += lax.dot_general(
-                chosen[:, m * pair : (m + 1) * pair], rr[k, :, pl.ds(strip, strip)], over_rows,
-                preferred_element_type=F32,
-            )
-
+    sum_tokens(PEERS // 2, PEERS)
     for c in range(4):
-        tok_out[:, pl.ds(c * strip, strip)] = acc[
-            c // 2, pl.ds(c % 2 * tok_count, tok_count), pl.ds(0, strip)
+        tok_out[:, pl.ds(c * strip, strip)] = sums[
+            c // 2, pl.ds(c % 2 * tok_count, tok_count)
         ].astype(BF16)
     terms = routed[...]
     for n in range(top_count):
@@ -595,6 +600,7 @@
             pltpu.VMEM((PEERS, SROWS, cols), BF16),
             pltpu.VMEM((2, PEERS, depth, cols), BF16),
             pltpu.VMEM((4, SROWS, SET * SROWS), BF16),
+            pltpu.VMEM((2, 2 * tok_count, strip), F32),
             pltpu.VMEM((PEERS, 4 * tok_count), F32),
             pltpu.VMEM((PEERS, tok_count), F32),
             pltpu.VMEM((PEERS, tok_count), F32),

time: 313 us -> 305 us (0.974); the launches traced: 307 us -> 305 us
  no operation moved by 1% of the time
where the time goes in v5:
time: 305 us
  Pallas kernels  292 us (96%)
  local copies, waits for them, and re-layouts  7.97 us (3%)
  other arithmetic  3.92 us (1%)
    pallas_call x1, Pallas kernels, local(): pl.pallas_call(layer_body, out_shape=[jax.ShapeDtypeStruct((3, PEERS, dep...  292 us
    slice x1, local copies, waits for them, and re-layouts, local(): grads[2:3]  6.59 us

profile of v5, /device:TPU:1, one launch (start us, length us, event | category | flops | bytes accessed | tf_op | source)
XLA Modules:
  0.0 304.6 jit_solution(4875496224627989284)
XLA Ops:
  0.7 1.4 select_reduce_fusion.order_ref
  2.1 1.3 convert_bitcast_fusion.gates_ref
  3.3 0.7 broadcast_in_dim.2.expert_ref
  4.0 292.0 %shard_map.119 = (bf16[3,32,128,384]{3,2,1,0:T(8,128)(2,1)}, bf16[32,144,256]{2,1,0:T(8,128)(2,1)}, bf16[128,1024]{1,0:T(8,128)(2,1)}, f32[8,128]{1,0:T(8,128)}) custom-call(s32[32]{0:T(128)} %select_reduce_fusion.order_ref, bf16[128,1024]{1,0:T(8,128)(2,1)} %tokens_ref.1, bf16[128,1024]{1,0:T(8,128)(2,1)} %cot_ref.1, ...), custom_call_target="tpu_custom_call" | custom-call | tf_op jit(solution)/shard_map/pallas_call | solution.py:575
  296.0 1.3 convert_bitcast_fusion.1
  297.3 0.0 copy-start
  297.3 6.6 %fusion.14 = (bf16[1,32,128,384]{3,2,1,0:T(8,128)(2,1)}, bf16[1,32,128,384]{3,2,1,0:T(8,128)(2,1)}, bf16[1,32,128,384]{3,2,1,0:T(8,128)(2,1)}) fusion(bf16[3,32,128,384]{3,2,1,0:T(8,128)(2,1)} %get-tuple-element.10), kind=kLoop, calls=%fused_computation.44 | loop fusion | bytes 18874368 | tf_op jit(solution)/shard_map/slice | solution.py:619
  303.9 0.0 copy-done
  303.9 0.7 copy.14
  (1 shorter events, 0.0 us)
Async XLA Ops:
  297.3 6.6 %copy-start = (bf16[128,1024]{1,0:T(8,128)(2,1)S(1)}, bf16[128,1024]{1,0:T(8,128)(2,1)}, u32[]{:S(2)}) copy-start(bf16[128,1024]{1,0:T(8,128)(2,1)} %get-tuple-element.19) | copy-start | bytes 786436

commit v6 on v5

--- a/solution.py
+++ b/solution.py
@@ -457,10 +457,10 @@
         for copy in out_copies(t):
             copy.start()
 
-    pl.loop(0, 4)(weight_grads)
+    pl.loop(0, 2)(weight_grads)
     combine(CHUNKS - 1)
     finish(CHUNKS - 2)
-    pl.loop(4, 6)(weight_grads)
+    pl.loop(2, 5)(weight_grads)
 
     for copy in q_copies:
         copy.wait_recv()
@@ -516,14 +516,14 @@
                     preferred_element_type=F32,
                 )
 
-    sum_tokens(0, PEERS // 2)
+    sum_tokens(0, PEERS - 2 * SET)
     finish(CHUNKS - 1)
-    pl.loop(6, 8)(weight_grads)
+    pl.loop(5, 8)(weight_grads)
     for t in (6, 7):
         for copy in out_copies(t):
             copy.wait()
 
-    sum_tokens(PEERS // 2, PEERS)
+    sum_tokens(PEERS - 2 * SET, PEERS)
     for c in range(4):
         tok_out[:, pl.ds(c * strip, strip)] = sums[
             c // 2, pl.ds(c % 2 * tok_count, tok_count)

time: 305 us -> 307 us (level)
  no operation moved by 1% of the time
where the time goes in v6:
time: 307 us
  Pallas kernels  294 us (96%)
  local copies, waits for them, and re-layouts  7.97 us (3%)
  other arithmetic  3.92 us (1%)
    pallas_call x1, Pallas kernels, local(): pl.pallas_call(layer_body, out_shape=[jax.ShapeDtypeStruct((3, PEERS, dep...  294 us
    slice x1, local copies, waits for them, and re-layouts, local(): grads[2:3]  6.59 us

profile of v6, /device:TPU:1, one launch (start us, length us, event | category | flops | bytes accessed | tf_op | source)
XLA Modules:
  0.0 306.7 jit_solution(6764944032389384276)
XLA Ops:
  0.7 1.4 select_reduce_fusion.order_ref
  2.1 1.3 convert_bitcast_fusion.gates_ref
  3.3 0.7 broadcast_in_dim.2.expert_ref
  4.0 294.2 %shard_map.119 = (bf16[3,32,128,384]{3,2,1,0:T(8,128)(2,1)}, bf16[32,144,256]{2,1,0:T(8,128)(2,1)}, bf16[128,1024]{1,0:T(8,128)(2,1)}, f32[8,128]{1,0:T(8,128)}) custom-call(s32[32]{0:T(128)} %select_reduce_fusion.order_ref, bf16[128,1024]{1,0:T(8,128)(2,1)} %tokens_ref.1, bf16[128,1024]{1,0:T(8,128)(2,1)} %cot_ref.1, ...), custom_call_target="tpu_custom_call" | custom-call | tf_op jit(solution)/shard_map/pallas_call | solution.py:575
  298.2 1.3 convert_bitcast_fusion.1
  299.4 0.0 copy-start
  299.4 6.6 %fusion.14 = (bf16[1,32,128,384]{3,2,1,0:T(8,128)(2,1)}, bf16[1,32,128,384]{3,2,1,0:T(8,128)(2,1)}, bf16[1,32,128,384]{3,2,1,0:T(8,128)(2,1)}) fusion(bf16[3,32,128,384]{3,2,1,0:T(8,128)(2,1)} %get-tuple-element.10), kind=kLoop, calls=%fused_computation.44 | loop fusion | bytes 18874368 | tf_op jit(solution)/shard_map/slice | solution.py:619
  306.0 0.0 copy-done
  306.0 0.7 copy.14
  (1 shorter events, 0.0 us)
Async XLA Ops:
  299.4 6.6 %copy-start = (bf16[128,1024]{1,0:T(8,128)(2,1)S(1)}, bf16[128,1024]{1,0:T(8,128)(2,1)}, u32[]{:S(2)}) copy-start(bf16[128,1024]{1,0:T(8,128)(2,1)} %get-tuple-element.19) | copy-start | bytes 786436
